TPU v7x, 32 devices: a whole 2x2x4 slice. The times are simulated.
32 devices in a mesh: fsdp: 16 (over z, y, x), seq: 2 (over core).
Axes of the slice: x: 2, y: 2, z: 4, core: 2. Of those that a mesh axis runs over, the one named last changes fastest.
Arguments:
- hidden_in: bfloat16 [16, 1024, 768], P('fsdp', 'seq'), may hold values from -6 to 6
- memory: bfloat16 [16, 1024, 768], P('fsdp', 'seq'), may hold values from -6 to 6
- target_ids: int32 [16, 1024], P('fsdp', 'seq'), may hold values from 0 to 4, never falling along the last dimension, each value on 1 to 512 neighbouring positions
- memory_ids: int32 [16, 1024], P('fsdp', 'seq'), may hold values from 0 to 4, never falling along the last dimension, each value on 1 to 512 neighbouring positions
- out_grad: bfloat16 [16, 1024, 768], P('fsdp', 'seq'), may hold values from -6 to 6
- self_query: bfloat16 [768, 768], P('fsdp'), may hold values from -0.21875 to 0.21875
- self_query_bias: bfloat16 [768], P('fsdp'), may hold values from -3 to 3
- self_key: bfloat16 [768, 768], P('fsdp'), may hold values from -0.21875 to 0.21875
- self_value: bfloat16 [768, 768], P('fsdp'), may hold values from -0.21875 to 0.21875
- self_value_bias: bfloat16 [768], P('fsdp'), may hold values from -3 to 3
- self_output: bfloat16 [768, 768], P('fsdp'), may hold values from -1.75 to 1.75
- self_output_bias: bfloat16 [768], P('fsdp'), may hold values from -3 to 3
- first_gain: bfloat16 [768], P('fsdp'), may hold values from 0.5 to 1.5
- first_shift: bfloat16 [768], P('fsdp'), may hold values from -3 to 3
- cross_query: bfloat16 [768, 768], P('fsdp'), may hold values from -0.21875 to 0.21875
- cross_query_bias: bfloat16 [768], P('fsdp'), may hold values from -3 to 3
- cross_key: bfloat16 [768, 768], P('fsdp'), may hold values from -0.21875 to 0.21875
- cross_value: bfloat16 [768, 768], P('fsdp'), may hold values from -0.21875 to 0.21875
- cross_value_bias: bfloat16 [768], P('fsdp'), may hold values from -3 to 3
- cross_output: bfloat16 [768, 768], P('fsdp'), may hold values from -1.75 to 1.75
- cross_output_bias: bfloat16 [768], P('fsdp'), may hold values from -3 to 3
- second_gain: bfloat16 [768], P('fsdp'), may hold values from 0.5 to 1.5
- second_shift: bfloat16 [768], P('fsdp'), may hold values from -3 to 3
- inner_weight: bfloat16 [768, 3072], P('fsdp'), may hold values from -0.21875 to 0.21875
- inner_bias: bfloat16 [3072], P('fsdp'), may hold values from -3 to 3
- outer_weight: bfloat16 [3072, 768], P('fsdp'), may hold values from -0.109375 to 0.109375
- outer_bias: bfloat16 [768], P('fsdp'), may hold values from -3 to 3
- third_gain: bfloat16 [768], P('fsdp'), may hold values from 0.5 to 1.5
- third_shift: bfloat16 [768], P('fsdp'), may hold values from -3 to 3
Outputs:
- layer_out: bfloat16 [16, 1024, 768], P('fsdp', 'seq')
- input_grad: bfloat16 [16, 1024, 768], P('fsdp', 'seq')
- memory_grad: bfloat16 [16, 1024, 768], P('fsdp', 'seq')
- self_query_grad: float32 [768, 768], P('fsdp')
- self_query_bias_grad: float32 [768], P('fsdp')
- self_key_grad: float32 [768, 768], P('fsdp')
- self_value_grad: float32 [768, 768], P('fsdp')
- self_value_bias_grad: float32 [768], P('fsdp')
- self_output_grad: float32 [768, 768], P('fsdp')
- self_output_bias_grad: float32 [768], P('fsdp')
- first_gain_grad: float32 [768], P('fsdp')
- first_shift_grad: float32 [768], P('fsdp')
- cross_query_grad: float32 [768, 768], P('fsdp')
- cross_query_bias_grad: float32 [768], P('fsdp')
- cross_key_grad: float32 [768, 768], P('fsdp')
- cross_value_grad: float32 [768, 768], P('fsdp')
- cross_value_bias_grad: float32 [768], P('fsdp')
- cross_output_grad: float32 [768, 768], P('fsdp')
- cross_output_bias_grad: float32 [768], P('fsdp')
- second_gain_grad: float32 [768], P('fsdp')
- second_shift_grad: float32 [768], P('fsdp')
- inner_weight_grad: float32 [768, 3072], P('fsdp')
- inner_bias_grad: float32 [3072], P('fsdp')
- outer_weight_grad: float32 [3072, 768], P('fsdp')
- outer_bias_grad: float32 [768], P('fsdp')
- third_gain_grad: float32 [768], P('fsdp')
- third_shift_grad: float32 [768], P('fsdp')
Inputs may be any that keep to these rules, and one draw needn't show every extreme that they name: `target_ids`: in each row the ids never fall and every id from 0 to 4 occurs; 0 is padding at the row's start; no id holds more than 512 positions of a row, and one of each row holds exactly that many. `memory_ids`: in each row the ids never fall and every id from 0 to 4 occurs; no id holds more than 512 positions of a row, and one of each row holds exactly that many.
All inputs are finite; a program needn't handle non-finite values.
Results may differ from a plain program's by a relative error of at most 0.025.
Values may be sent and summed in bfloat16 or wider, within the bound.
A program may use at most 192 MiB of HBM per device.

v0:
```python
import math

import jax
import jax.numpy as jnp
from jax import lax
from jax.sharding import PartitionSpec as P

HEAD_DIM = 64


eps_norm = 1e-05
masked_score = -1e30


def dense(left, right):
    return jnp.dot(left, right, preferred_element_type=jnp.float32)


def dense_back(left, right):
    return lax.dot_general(
        left, right, (((1,), (1,)), ((), ())), preferred_element_type=jnp.float32
    )


def dense_grad(left, right):
    return lax.dot_general(
        left, right, (((0,), (0,)), ((), ())), preferred_element_type=jnp.float32
    )


def column_sum(values):
    return jnp.sum(values, axis=0, dtype=jnp.float32)


def layer_norm(resid, gain, shift):
    center = resid - jnp.mean(resid, axis=-1, keepdims=True)
    spread = jnp.mean(center * center, axis=-1, keepdims=True)
    inverse = lax.rsqrt(spread + eps_norm)
    normed = center * inverse
    return (normed * gain.astype(jnp.float32) + shift.astype(jnp.float32), normed, inverse)


def norm_back(upstream, normed, inverse, gain):
    scaled = upstream * gain.astype(jnp.float32)
    plain_mean = jnp.mean(scaled, axis=-1, keepdims=True)
    cross_mean = jnp.mean(scaled * normed, axis=-1, keepdims=True)
    result = inverse * (scaled - plain_mean - normed * cross_mean)
    return (result, jnp.sum(upstream * normed, axis=0), jnp.sum(upstream, axis=0))


def head_slice(array, start, span):
    piece = lax.dynamic_slice_in_dim(array, start, span, 2)
    return piece.reshape(array.shape[0], array.shape[1], 2, span // 2)


def attend_forward(query, keys, values, allowed):
    rows, length, width = query.shape
    span = 2 * HEAD_DIM
    pairs = width // span

    def one_pair(index, carry):
        mixed, logsum = carry
        start = index * span
        query_part = head_slice(query, start, span)
        key_part = head_slice(keys, start, span)
        value_part = head_slice(values, start, span)
        scores = jnp.einsum(
            "rqhe,rkhe->rhqk", query_part, key_part, preferred_element_type=jnp.float32
        )
        scores = jnp.where(allowed[:, None], scores, masked_score)
        highest = jnp.max(scores, axis=-1, keepdims=True)
        exponent = jnp.exp(scores - highest)
        total = jnp.sum(exponent, axis=-1, keepdims=True)
        probs = (exponent / total).astype(jnp.bfloat16)
        part = jnp.einsum("rhqk,rkhe->rqhe", probs, value_part, preferred_element_type=jnp.float32)
        mixed = lax.dynamic_update_slice_in_dim(mixed, part.reshape(rows, length, span), start, 2)
        logsum = lax.dynamic_update_slice_in_dim(
            logsum, (highest + jnp.log(total))[None, :, :, :, 0], index, 0
        )
        return (mixed, logsum)

    mixed = jnp.zeros((rows, length, width), jnp.float32)
    logsum = jnp.zeros((pairs, rows, 2, length), jnp.float32)
    return lax.fori_loop(0, pairs, one_pair, (mixed, logsum))


def attend_backward(query, keys, values, allowed, logsum, grad_mixed):
    rows, length, width = query.shape
    extent = keys.shape[1]
    span = 2 * HEAD_DIM
    pairs = width // span

    def one_pair(index, carry):
        start = index * span
        query_part = head_slice(query, start, span)
        key_part = head_slice(keys, start, span)
        value_part = head_slice(values, start, span)
        grad_part = head_slice(grad_mixed, start, span)
        scores = jnp.einsum(
            "rqhe,rkhe->rhqk", query_part, key_part, preferred_element_type=jnp.float32
        )
        scores = jnp.where(allowed[:, None], scores, masked_score)
        pair_logsum = lax.dynamic_index_in_dim(logsum, index, 0, keepdims=False)
        probs = jnp.exp(scores - pair_logsum[..., None])
        prob_grad = jnp.einsum(
            "rqhe,rkhe->rhqk", grad_part, value_part, preferred_element_type=jnp.float32
        )
        row_total = jnp.sum(probs * prob_grad, axis=-1, keepdims=True)
        score_grad = (probs * (prob_grad - row_total)).astype(jnp.bfloat16)
        query_grad = jnp.einsum(
            "rhqk,rkhe->rqhe", score_grad, key_part, preferred_element_type=jnp.float32
        )
        grad_query = lax.dynamic_update_slice_in_dim(
            carry[0], query_grad.reshape(rows, length, span), start, 2
        )
        row_sums = lax.dynamic_update_slice_in_dim(carry[1], row_total[None, :, :, :, 0], index, 0)
        probs_low = probs.astype(jnp.bfloat16)
        value_grad = jnp.einsum(
            "rhqk,rqhe->rkhe", probs_low, grad_part, preferred_element_type=jnp.float32
        )
        key_grad = jnp.einsum(
            "rhqk,rqhe->rkhe", score_grad, query_part, preferred_element_type=jnp.float32
        )
        grad_keys = lax.dynamic_update_slice_in_dim(
            carry[2], key_grad.reshape(rows, extent, span), start, 2
        )
        grad_values = lax.dynamic_update_slice_in_dim(
            carry[3], value_grad.reshape(rows, extent, span), start, 2
        )
        return (grad_query, row_sums, grad_keys, grad_values)

    start_query = jnp.zeros((rows, length, width), jnp.float32)
    start_sums = jnp.zeros((pairs, rows, 2, length), jnp.float32)
    start_keys = jnp.zeros((rows, extent, width), jnp.float32)
    return lax.fori_loop(0, pairs, one_pair, (start_query, start_sums, start_keys, start_keys))


def body(
    hidden_in,
    memory,
    target_ids,
    memory_ids,
    out_grad,
    self_query,
    self_query_bias,
    self_key,
    self_value,
    self_value_bias,
    self_output,
    self_output_bias,
    first_gain,
    first_shift,
    cross_query,
    cross_query_bias,
    cross_key,
    cross_value,
    cross_value_bias,
    cross_output,
    cross_output_bias,
    second_gain,
    second_shift,
    inner_weight,
    inner_bias,
    outer_weight,
    outer_bias,
    third_gain,
    third_shift,
):
    (
        whole_self_query,
        whole_self_query_bias,
        whole_self_key,
        whole_self_value,
        whole_self_value_bias,
        whole_self_output,
        whole_self_output_bias,
        whole_first_gain,
        whole_first_shift,
        whole_cross_query,
        whole_cross_query_bias,
        whole_cross_key,
        whole_cross_value,
        whole_cross_value_bias,
        whole_cross_output,
        whole_cross_output_bias,
        whole_second_gain,
        whole_second_shift,
        whole_inner_weight,
        whole_inner_bias,
        whole_outer_weight,
        whole_outer_bias,
        whole_third_gain,
        whole_third_shift,
    ) = (
        lax.all_gather(self_query, "fsdp", axis=0, tiled=True),
        lax.all_gather(self_query_bias, "fsdp", axis=0, tiled=True),
        lax.all_gather(self_key, "fsdp", axis=0, tiled=True),
        lax.all_gather(self_value, "fsdp", axis=0, tiled=True),
        lax.all_gather(self_value_bias, "fsdp", axis=0, tiled=True),
        lax.all_gather(self_output, "fsdp", axis=0, tiled=True),
        lax.all_gather(self_output_bias, "fsdp", axis=0, tiled=True),
        lax.all_gather(first_gain, "fsdp", axis=0, tiled=True),
        lax.all_gather(first_shift, "fsdp", axis=0, tiled=True),
        lax.all_gather(cross_query, "fsdp", axis=0, tiled=True),
        lax.all_gather(cross_query_bias, "fsdp", axis=0, tiled=True),
        lax.all_gather(cross_key, "fsdp", axis=0, tiled=True),
        lax.all_gather(cross_value, "fsdp", axis=0, tiled=True),
        lax.all_gather(cross_value_bias, "fsdp", axis=0, tiled=True),
        lax.all_gather(cross_output, "fsdp", axis=0, tiled=True),
        lax.all_gather(cross_output_bias, "fsdp", axis=0, tiled=True),
        lax.all_gather(second_gain, "fsdp", axis=0, tiled=True),
        lax.all_gather(second_shift, "fsdp", axis=0, tiled=True),
        lax.all_gather(inner_weight, "fsdp", axis=0, tiled=True),
        lax.all_gather(inner_bias, "fsdp", axis=0, tiled=True),
        lax.all_gather(outer_weight, "fsdp", axis=0, tiled=True),
        lax.all_gather(outer_bias, "fsdp", axis=0, tiled=True),
        lax.all_gather(third_gain, "fsdp", axis=0, tiled=True),
        lax.all_gather(third_shift, "fsdp", axis=0, tiled=True),
    )
    rows, length, width = hidden_in.shape
    tokens = rows * length
    scale = HEAD_DIM ** (-0.5)
    flat_in = hidden_in.reshape(tokens, width)
    flat_memory = memory.reshape(tokens, width)
    target_marks = target_ids.astype(jnp.bfloat16)
    memory_marks = memory_ids.astype(jnp.bfloat16)
    key_two = dense(flat_memory, whole_cross_key).astype(jnp.bfloat16).reshape(rows, length, width)
    value_two = (
        (dense(flat_memory, whole_cross_value) + whole_cross_value_bias.astype(jnp.float32))
        .astype(jnp.bfloat16)
        .reshape(rows, length, width)
    )
    keys_two, values_two, source_marks = (
        lax.all_gather(key_two, "seq", axis=1, tiled=True),
        lax.all_gather(value_two, "seq", axis=1, tiled=True),
        lax.all_gather(memory_marks, "seq", axis=1, tiled=True),
    )
    allowed_cross = target_marks[:, :, None] == source_marks[:, None, :]
    query_one = (
        ((dense(flat_in, whole_self_query) + whole_self_query_bias.astype(jnp.float32)) * scale)
        .astype(jnp.bfloat16)
        .reshape(rows, length, width)
    )
    key_one = dense(flat_in, whole_self_key).astype(jnp.bfloat16).reshape(rows, length, width)
    value_one = (
        (dense(flat_in, whole_self_value) + whole_self_value_bias.astype(jnp.float32))
        .astype(jnp.bfloat16)
        .reshape(rows, length, width)
    )
    keys_one, values_one, key_marks = (
        lax.all_gather(key_one, "seq", axis=1, tiled=True),
        lax.all_gather(value_one, "seq", axis=1, tiled=True),
        lax.all_gather(target_marks, "seq", axis=1, tiled=True),
    )
    query_places = lax.axis_index("seq") * length + jnp.arange(length)
    key_places = jnp.arange(keys_one.shape[1])
    allowed_self = (target_marks[:, :, None] == key_marks[:, None, :]) & (
        key_places[None, None, :] <= query_places[None, :, None]
    )
    mixed_one, logsum_one = attend_forward(query_one, keys_one, values_one, allowed_self)
    mixed_one = mixed_one.astype(jnp.bfloat16).reshape(tokens, width)
    resid_one = (
        flat_in.astype(jnp.float32)
        + dense(mixed_one, whole_self_output)
        + whole_self_output_bias.astype(jnp.float32)
    )
    first, normed_one, inverse_one = layer_norm(resid_one, whole_first_gain, whole_first_shift)
    first = first.astype(jnp.bfloat16)
    query_two = (
        ((dense(first, whole_cross_query) + whole_cross_query_bias.astype(jnp.float32)) * scale)
        .astype(jnp.bfloat16)
        .reshape(rows, length, width)
    )
    mixed_two, logsum_two = attend_forward(query_two, keys_two, values_two, allowed_cross)
    mixed_two = mixed_two.astype(jnp.bfloat16).reshape(tokens, width)
    resid_two = (
        first.astype(jnp.float32)
        + dense(mixed_two, whole_cross_output)
        + whole_cross_output_bias.astype(jnp.float32)
    )
    second, normed_two, inverse_two = layer_norm(resid_two, whole_second_gain, whole_second_shift)
    second = second.astype(jnp.bfloat16)
    inner = dense(second, whole_inner_weight) + whole_inner_bias.astype(jnp.float32)
    active = jax.nn.gelu(inner, approximate=False).astype(jnp.bfloat16)
    resid_three = (
        second.astype(jnp.float32)
        + dense(active, whole_outer_weight)
        + whole_outer_bias.astype(jnp.float32)
    )
    final, normed_three, inverse_three = layer_norm(
        resid_three, whole_third_gain, whole_third_shift
    )
    layer_out = final.astype(jnp.bfloat16).reshape(rows, length, width)
    (
        whole_self_query,
        whole_self_key,
        whole_self_value,
        whole_self_output,
        whole_first_gain,
        whole_cross_query,
        whole_cross_key,
        whole_cross_value,
        whole_cross_output,
        whole_second_gain,
        whole_inner_weight,
        whole_outer_weight,
        whole_third_gain,
    ) = (
        lax.all_gather(self_query, "fsdp", axis=0, tiled=True),
        lax.all_gather(self_key, "fsdp", axis=0, tiled=True),
        lax.all_gather(self_value, "fsdp", axis=0, tiled=True),
        lax.all_gather(self_output, "fsdp", axis=0, tiled=True),
        lax.all_gather(first_gain, "fsdp", axis=0, tiled=True),
        lax.all_gather(cross_query, "fsdp", axis=0, tiled=True),
        lax.all_gather(cross_key, "fsdp", axis=0, tiled=True),
        lax.all_gather(cross_value, "fsdp", axis=0, tiled=True),
        lax.all_gather(cross_output, "fsdp", axis=0, tiled=True),
        lax.all_gather(second_gain, "fsdp", axis=0, tiled=True),
        lax.all_gather(inner_weight, "fsdp", axis=0, tiled=True),
        lax.all_gather(outer_weight, "fsdp", axis=0, tiled=True),
        lax.all_gather(third_gain, "fsdp", axis=0, tiled=True),
    )
    keep = (target_ids > 0).astype(jnp.float32).reshape(tokens, 1)
    upstream = out_grad.reshape(tokens, width).astype(jnp.float32) * keep
    grad_three, grad_third_gain, grad_third_shift = norm_back(
        upstream, normed_three, inverse_three, whole_third_gain
    )
    grad_outer = grad_three.astype(jnp.bfloat16)
    grad_outer_bias = column_sum(grad_outer)
    grad_outer_weight = dense_grad(active, grad_outer)
    grad_active = dense_back(grad_outer, whole_outer_weight)
    cumulative = 0.5 * (1.0 + lax.erf(inner * math.sqrt(0.5)))
    density = jnp.exp(-0.5 * inner * inner) * (1.0 / math.sqrt(2.0 * math.pi))
    grad_inner = (grad_active * (cumulative + inner * density)).astype(jnp.bfloat16)
    grad_inner_bias = column_sum(grad_inner)
    grad_inner_weight = dense_grad(second, grad_inner)
    grad_second = grad_three + dense_back(grad_inner, whole_inner_weight)
    grad_two, grad_second_gain, grad_second_shift = norm_back(
        grad_second, normed_two, inverse_two, whole_second_gain
    )
    branch_two = grad_two.astype(jnp.bfloat16)
    grad_cross_output_bias = column_sum(branch_two)
    grad_cross_output = dense_grad(mixed_two, branch_two)
    grad_mixed_two = (
        dense_back(branch_two, whole_cross_output).astype(jnp.bfloat16).reshape(rows, length, width)
    )
    query_sum_two, sums_two, key_sum_two, value_sum_two = attend_backward(
        query_two, keys_two, values_two, allowed_cross, logsum_two, grad_mixed_two
    )
    key_local_two, value_local_two = (
        lax.psum_scatter(
            key_sum_two.astype(jnp.bfloat16), "seq", scatter_dimension=1, tiled=True
        ).astype(jnp.float32),
        lax.psum_scatter(
            value_sum_two.astype(jnp.bfloat16), "seq", scatter_dimension=1, tiled=True
        ).astype(jnp.float32),
    )
    key_grad_two = key_local_two.astype(jnp.bfloat16).reshape(tokens, width)
    value_grad_two = value_local_two.astype(jnp.bfloat16).reshape(tokens, width)
    query_grad_two = (query_sum_two.astype(jnp.bfloat16) * scale).reshape(tokens, width)
    grad_cross_query = dense_grad(first, query_grad_two)
    grad_cross_query_bias = column_sum(query_grad_two)
    grad_cross_key = dense_grad(flat_memory, key_grad_two)
    grad_cross_value = dense_grad(flat_memory, value_grad_two)
    grad_cross_value_bias = column_sum(value_grad_two)
    memory_grad = (
        (dense_back(key_grad_two, whole_cross_key) + dense_back(value_grad_two, whole_cross_value))
        .astype(jnp.bfloat16)
        .reshape(rows, length, width)
    )
    grad_first = grad_two + dense_back(query_grad_two, whole_cross_query)
    grad_one, grad_first_gain, grad_first_shift = norm_back(
        grad_first, normed_one, inverse_one, whole_first_gain
    )
    branch_one = grad_one.astype(jnp.bfloat16)
    grad_self_output_bias = column_sum(branch_one)
    grad_self_output = dense_grad(mixed_one, branch_one)
    grad_mixed_one = (
        dense_back(branch_one, whole_self_output).astype(jnp.bfloat16).reshape(rows, length, width)
    )
    query_sum_one, sums_one, key_sum_one, value_sum_one = attend_backward(
        query_one, keys_one, values_one, allowed_self, logsum_one, grad_mixed_one
    )
    key_local_one, value_local_one = (
        lax.psum_scatter(
            key_sum_one.astype(jnp.bfloat16), "seq", scatter_dimension=1, tiled=True
        ).astype(jnp.float32),
        lax.psum_scatter(
            value_sum_one.astype(jnp.bfloat16), "seq", scatter_dimension=1, tiled=True
        ).astype(jnp.float32),
    )
    key_grad_one = key_local_one.astype(jnp.bfloat16).reshape(tokens, width)
    value_grad_one = value_local_one.astype(jnp.bfloat16).reshape(tokens, width)
    query_grad_one = (query_sum_one.astype(jnp.bfloat16) * scale).reshape(tokens, width)
    grad_self_query = dense_grad(flat_in, query_grad_one)
    grad_self_query_bias = column_sum(query_grad_one)
    grad_self_key = dense_grad(flat_in, key_grad_one)
    grad_self_value = dense_grad(flat_in, value_grad_one)
    grad_self_value_bias = column_sum(value_grad_one)
    input_total = (
        grad_one
        + dense_back(query_grad_one, whole_self_query)
        + dense_back(key_grad_one, whole_self_key)
        + dense_back(value_grad_one, whole_self_value)
    )
    input_grad = input_total.astype(jnp.bfloat16).reshape(rows, length, width)
    (
        grad_self_query,
        grad_self_query_bias,
        grad_self_key,
        grad_self_value,
        grad_self_value_bias,
        grad_self_output,
        grad_self_output_bias,
        grad_first_gain,
        grad_first_shift,
        grad_cross_query,
        grad_cross_query_bias,
        grad_cross_key,
        grad_cross_value,
        grad_cross_value_bias,
        grad_cross_output,
        grad_cross_output_bias,
        grad_second_gain,
        grad_second_shift,
        grad_inner_weight,
        grad_inner_bias,
        grad_outer_weight,
        grad_outer_bias,
        grad_third_gain,
        grad_third_shift,
    ) = (
        lax.psum_scatter(
            grad_self_query.astype(jnp.bfloat16), "fsdp", scatter_dimension=0, tiled=True
        ).astype(jnp.float32),
        lax.psum_scatter(
            grad_self_query_bias.astype(jnp.bfloat16), "fsdp", scatter_dimension=0, tiled=True
        ).astype(jnp.float32),
        lax.psum_scatter(
            grad_self_key.astype(jnp.bfloat16), "fsdp", scatter_dimension=0, tiled=True
        ).astype(jnp.float32),
        lax.psum_scatter(
            grad_self_value.astype(jnp.bfloat16), "fsdp", scatter_dimension=0, tiled=True
        ).astype(jnp.float32),
        lax.psum_scatter(
            grad_self_value_bias.astype(jnp.bfloat16), "fsdp", scatter_dimension=0, tiled=True
        ).astype(jnp.float32),
        lax.psum_scatter(
            grad_self_output.astype(jnp.bfloat16), "fsdp", scatter_dimension=0, tiled=True
        ).astype(jnp.float32),
        lax.psum_scatter(
            grad_self_output_bias.astype(jnp.bfloat16), "fsdp", scatter_dimension=0, tiled=True
        ).astype(jnp.float32),
        lax.psum_scatter(
            grad_first_gain.astype(jnp.bfloat16), "fsdp", scatter_dimension=0, tiled=True
        ).astype(jnp.float32),
        lax.psum_scatter(
            grad_first_shift.astype(jnp.bfloat16), "fsdp", scatter_dimension=0, tiled=True
        ).astype(jnp.float32),
        lax.psum_scatter(
            grad_cross_query.astype(jnp.bfloat16), "fsdp", scatter_dimension=0, tiled=True
        ).astype(jnp.float32),
        lax.psum_scatter(
            grad_cross_query_bias.astype(jnp.bfloat16), "fsdp", scatter_dimension=0, tiled=True
        ).astype(jnp.float32),
        lax.psum_scatter(
            grad_cross_key.astype(jnp.bfloat16), "fsdp", scatter_dimension=0, tiled=True
        ).astype(jnp.float32),
        lax.psum_scatter(
            grad_cross_value.astype(jnp.bfloat16), "fsdp", scatter_dimension=0, tiled=True
        ).astype(jnp.float32),
        lax.psum_scatter(
            grad_cross_value_bias.astype(jnp.bfloat16), "fsdp", scatter_dimension=0, tiled=True
        ).astype(jnp.float32),
        lax.psum_scatter(
            grad_cross_output.astype(jnp.bfloat16), "fsdp", scatter_dimension=0, tiled=True
        ).astype(jnp.float32),
        lax.psum_scatter(
            grad_cross_output_bias.astype(jnp.bfloat16), "fsdp", scatter_dimension=0, tiled=True
        ).astype(jnp.float32),
        lax.psum_scatter(
            grad_second_gain.astype(jnp.bfloat16), "fsdp", scatter_dimension=0, tiled=True
        ).astype(jnp.float32),
        lax.psum_scatter(
            grad_second_shift.astype(jnp.bfloat16), "fsdp", scatter_dimension=0, tiled=True
        ).astype(jnp.float32),
        lax.psum_scatter(
            grad_inner_weight.astype(jnp.bfloat16), "fsdp", scatter_dimension=0, tiled=True
        ).astype(jnp.float32),
        lax.psum_scatter(
            grad_inner_bias.astype(jnp.bfloat16), "fsdp", scatter_dimension=0, tiled=True
        ).astype(jnp.float32),
        lax.psum_scatter(
            grad_outer_weight.astype(jnp.bfloat16), "fsdp", scatter_dimension=0, tiled=True
        ).astype(jnp.float32),
        lax.psum_scatter(
            grad_outer_bias.astype(jnp.bfloat16), "fsdp", scatter_dimension=0, tiled=True
        ).astype(jnp.float32),
        lax.psum_scatter(
            grad_third_gain.astype(jnp.bfloat16), "fsdp", scatter_dimension=0, tiled=True
        ).astype(jnp.float32),
        lax.psum_scatter(
            grad_third_shift.astype(jnp.bfloat16), "fsdp", scatter_dimension=0, tiled=True
        ).astype(jnp.float32),
    )
    (
        grad_self_query,
        grad_self_query_bias,
        grad_self_key,
        grad_self_value,
        grad_self_value_bias,
        grad_self_output,
        grad_self_output_bias,
        grad_first_gain,
        grad_first_shift,
        grad_cross_query,
        grad_cross_query_bias,
        grad_cross_key,
        grad_cross_value,
        grad_cross_value_bias,
        grad_cross_output,
        grad_cross_output_bias,
        grad_second_gain,
        grad_second_shift,
        grad_inner_weight,
        grad_inner_bias,
        grad_outer_weight,
        grad_outer_bias,
        grad_third_gain,
        grad_third_shift,
    ) = (
        lax.psum(grad_self_query.astype(jnp.bfloat16), "seq").astype(jnp.float32),
        lax.psum(grad_self_query_bias.astype(jnp.bfloat16), "seq").astype(jnp.float32),
        lax.psum(grad_self_key.astype(jnp.bfloat16), "seq").astype(jnp.float32),
        lax.psum(grad_self_value.astype(jnp.bfloat16), "seq").astype(jnp.float32),
        lax.psum(grad_self_value_bias.astype(jnp.bfloat16), "seq").astype(jnp.float32),
        lax.psum(grad_self_output.astype(jnp.bfloat16), "seq").astype(jnp.float32),
        lax.psum(grad_self_output_bias.astype(jnp.bfloat16), "seq").astype(jnp.float32),
        lax.psum(grad_first_gain.astype(jnp.bfloat16), "seq").astype(jnp.float32),
        lax.psum(grad_first_shift.astype(jnp.bfloat16), "seq").astype(jnp.float32),
        lax.psum(grad_cross_query.astype(jnp.bfloat16), "seq").astype(jnp.float32),
        lax.psum(grad_cross_query_bias.astype(jnp.bfloat16), "seq").astype(jnp.float32),
        lax.psum(grad_cross_key.astype(jnp.bfloat16), "seq").astype(jnp.float32),
        lax.psum(grad_cross_value.astype(jnp.bfloat16), "seq").astype(jnp.float32),
        lax.psum(grad_cross_value_bias.astype(jnp.bfloat16), "seq").astype(jnp.float32),
        lax.psum(grad_cross_output.astype(jnp.bfloat16), "seq").astype(jnp.float32),
        lax.psum(grad_cross_output_bias.astype(jnp.bfloat16), "seq").astype(jnp.float32),
        lax.psum(grad_second_gain.astype(jnp.bfloat16), "seq").astype(jnp.float32),
        lax.psum(grad_second_shift.astype(jnp.bfloat16), "seq").astype(jnp.float32),
        lax.psum(grad_inner_weight.astype(jnp.bfloat16), "seq").astype(jnp.float32),
        lax.psum(grad_inner_bias.astype(jnp.bfloat16), "seq").astype(jnp.float32),
        lax.psum(grad_outer_weight.astype(jnp.bfloat16), "seq").astype(jnp.float32),
        lax.psum(grad_outer_bias.astype(jnp.bfloat16), "seq").astype(jnp.float32),
        lax.psum(grad_third_gain.astype(jnp.bfloat16), "seq").astype(jnp.float32),
        lax.psum(grad_third_shift.astype(jnp.bfloat16), "seq").astype(jnp.float32),
    )
    return (
        layer_out,
        input_grad,
        memory_grad,
        grad_self_query,
        grad_self_query_bias,
        grad_self_key,
        grad_self_value,
        grad_self_value_bias,
        grad_self_output,
        grad_self_output_bias,
        grad_first_gain,
        grad_first_shift,
        grad_cross_query,
        grad_cross_query_bias,
        grad_cross_key,
        grad_cross_value,
        grad_cross_value_bias,
        grad_cross_output,
        grad_cross_output_bias,
        grad_second_gain,
        grad_second_shift,
        grad_inner_weight,
        grad_inner_bias,
        grad_outer_weight,
        grad_outer_bias,
        grad_third_gain,
        grad_third_shift,
    )


def solution(mesh):
    return jax.shard_map(
        body,
        mesh=mesh,
        in_specs=(
            P("fsdp", "seq", None),
            P("fsdp", "seq", None),
            P("fsdp", "seq"),
            P("fsdp", "seq"),
            P("fsdp", "seq", None),
            P("fsdp", None),
            P("fsdp"),
            P("fsdp", None),
            P("fsdp", None),
            P("fsdp"),
            P("fsdp", None),
            P("fsdp"),
            P("fsdp"),
            P("fsdp"),
            P("fsdp", None),
            P("fsdp"),
            P("fsdp", None),
            P("fsdp", None),
            P("fsdp"),
            P("fsdp", None),
            P("fsdp"),
            P("fsdp"),
            P("fsdp"),
            P("fsdp", None),
            P("fsdp"),
            P("fsdp", None),
            P("fsdp"),
            P("fsdp"),
            P("fsdp"),
        ),
        out_specs=(
            P("fsdp", "seq", None),
            P("fsdp", "seq", None),
            P("fsdp", "seq", None),
            P("fsdp", None),
            P("fsdp"),
            P("fsdp", None),
            P("fsdp", None),
            P("fsdp"),
            P("fsdp", None),
            P("fsdp"),
            P("fsdp"),
            P("fsdp"),
            P("fsdp", None),
            P("fsdp"),
            P("fsdp", None),
            P("fsdp", None),
            P("fsdp"),
            P("fsdp", None),
            P("fsdp"),
            P("fsdp"),
            P("fsdp"),
            P("fsdp", None),
            P("fsdp"),
            P("fsdp", None),
            P("fsdp"),
            P("fsdp"),
            P("fsdp"),
        ),
        check_vma=False,
    )
```

profile of v0, /device:TPU:0, one launch (start us, length us, event | category | flops | bytes accessed | tf_op | source)
XLA Modules:
  0.0 2325.6 jit_solution(2936554314455072338)
XLA Ops:
  24.2 78.9 %all-reduce.29 = (bf16[768]{0:T(1024)(128)(2,1)S(1)}, bf16[768]{0:T(1024)(128)(2,1)S(1)}, bf16[768]{0:T(1024)(128)(2,1)S(1)}, bf16[768]{0:T(1024)(128)(2,1)S(1)}...) all-reduce(bf16[768]{0:T(1024)(128)(2,1)S(1)} %dynamic-update-slice, ...), channel_id=1, replica_groups=mesh['fsdp'=16,'seq'=2] {'fsdp'}, use_global_device_ids=true, to_apply=%add.1 | all-reduce | flops 12288 | bytes 49152
  106.4 21.4 all-gather.23.cloned.1.call-done
  132.3 53.3 %all-gather.27.cloned.1.call-done = bf16[768,768]{1,0:T(8,128)(2,1)} async-done(((bf16[48,768]{1,0:T(8,128)(2,1)}), bf16[768,768]{1,0:T(8,128)(2,1)}) %all-gather.27.cloned.1.call-update) | async-done | bytes 1179664 | tf_op jit(solution)/shard_map/all_gather | solution.py:207
  188.7 54.7 %all-gather.31.cloned.1.call-done = bf16[768,768]{1,0:T(8,128)(2,1)} async-done(((bf16[48,768]{1,0:T(8,128)(2,1)}), bf16[768,768]{1,0:T(8,128)(2,1)}) %all-gather.31.cloned.1.call-update) | async-done | bytes 1179664 | tf_op jit(solution)/shard_map/all_gather | solution.py:206
  255.0 46.1 %all-gather.21.cloned.1.call-done = bf16[768,768]{1,0:T(8,128)(2,1)} async-done(((bf16[48,768]{1,0:T(8,128)(2,1)}), bf16[768,768]{1,0:T(8,128)(2,1)}) %all-gather.21.cloned.1.call-update) | async-done | bytes 1179664 | tf_op jit(solution)/shard_map/all_gather | solution.py:195
  303.3 8.4 all-gather.39.cloned.1.call-done
  313.9 10.9 all-gather.41.cloned.1.call-done
  328.4 34.7 %while.68 = (s32[]{:T(128)}, bf16[1,512,768]{1,2,0:T(8,128)(2,1)}, f32[6,1,2,512]{3,2,1,0:T(2,128)S(1)}, bf16[1,1024,768]{1,2,0:T(8,128)(2,1)S(1)}, bf16[1,512,7...) while((s32[]{:T(128)}, bf16[1,512,768]{1,2,0:T(8,128)(2,1)}, ...), condition=%wide.region_3.4_spmd.clone, body=%wide.region_0.3_spmd.clone.sunk | while | flops 280493056 | bytes 17077436 | solution.py:84
  363.1 21.9 all-gather.25.cloned.1.call-done
  389.2 53.6 %all-gather.29.cloned.1.call-done = bf16[768,768]{1,0:T(8,128)(2,1)} async-done(((bf16[48,768]{1,0:T(8,128)(2,1)}), bf16[768,768]{1,0:T(8,128)(2,1)}) %all-gather.29.cloned.1.call-update) | async-done | bytes 1179664 | tf_op jit(solution)/shard_map/all_gather | solution.py:204
  445.2 8.3 all-gather.43.cloned.1.call-done
  455.3 10.8 all-gather.45.cloned.1.call-done
  470.3 36.7 %while.69 = (s32[]{:T(128)}, bf16[1,512,768]{1,2,0:T(8,128)(2,1)}, f32[6,1,2,512]{3,2,1,0:T(2,128)}, bf16[1,1024,768]{1,2,0:T(8,128)(2,1)S(1)}, bf16[1,512,768]{...) while((s32[]{:T(128)}, bf16[1,512,768]{1,2,0:T(8,128)(2,1)}, ...), condition=%wide.region_9.10_spmd.clone, body=%wide.region_6.9_spmd.clone.sunk | while | flops 278395904 | bytes 17075888 | solution.py:84
  507.1 19.1 all-gather.33.cloned.1.call-done
  530.3 78.0 %all-gather.35.cloned.1.call-done = bf16[768,3072]{1,0:T(8,128)(2,1)} async-done(((bf16[48,3072]{1,0:T(8,128)(2,1)}), bf16[768,3072]{1,0:T(8,128)(2,1)}) %all-gather.35.cloned.1.call-update) | async-done | bytes 4718608 | tf_op jit(solution)/shard_map/all_gather | solution.py:213
  608.3 20.3 fusion.34
  628.6 61.4 %all-gather.37.cloned.1.call-done = bf16[3072,768]{1,0:T(8,128)(2,1)} async-done(((bf16[192,768]{1,0:T(8,128)(2,1)}), bf16[3072,768]{1,0:T(8,128)(2,1)}) %all-gather.37.cloned.1.call-update) | async-done | bytes 4718608 | tf_op jit(solution)/shard_map/all_gather | solution.py:215
  690.1 6.2 fusion.115
  700.7 5.6 fusion.116
  716.6 98.1 %while.70 = (s32[]{:T(128)}, bf16[1,512,768]{1,2,0:T(8,128)(2,1)}, bf16[1,1024,768]{1,2,0:T(8,128)(2,1)}, bf16[1,1024,768]{1,2,0:T(8,128)(2,1)}, bf16[1,1024,768...) while((s32[]{:T(128)}, bf16[1,512,768]{1,2,0:T(8,128)(2,1)}, ...), condition=%wide.region_20.21_spmd.clone, body=%wide.region_18.0_spmd.clone.sunk | while | flops 684194816 | bytes 61766952 | solution.py:135
  723.8 4.0 multiply_reduce_fusion.13
  740.0 4.0 multiply_reduce_fusion.13
  756.3 4.0 multiply_reduce_fusion.13
  772.5 4.0 multiply_reduce_fusion.13
  788.8 4.0 multiply_reduce_fusion.13
  805.1 4.0 multiply_reduce_fusion.13
  825.1 103.0 %while.71 = (s32[]{:T(128)}, bf16[1,512,768]{1,2,0:T(8,128)(2,1)}, bf16[1,1024,768]{1,2,0:T(8,128)(2,1)}, bf16[1,1024,768]{1,2,0:T(8,128)(2,1)}, bf16[1,1024,768...) while((s32[]{:T(128)}, bf16[1,512,768]{1,2,0:T(8,128)(2,1)}, ...), condition=%wide.region_25.26_spmd.clone, body=%wide.region_23.0_spmd.clone.sunk | while | flops 686291968 | bytes 55477496 | solution.py:135
  833.0 4.0 multiply_reduce_fusion.14
  850.2 4.0 multiply_reduce_fusion.14
  867.4 4.0 multiply_reduce_fusion.14
  918.9 4.0 multiply_reduce_fusion.14
  941.7 6.7 reduce-scatter.27.cloned.1.call-done
  954.1 6.8 reduce-scatter.29.cloned.1.call-done
  966.5 6.9 reduce-scatter.31.cloned.1.call-done
  988.8 6.5 convolution_convert_fusion.1
  996.7 6.7 convolution_convert_fusion
  1010.3 93.3 %reduce-scatter.43.cloned.1.call-done = bf16[48,768]{1,0:T(8,128)(2,1)} async-done(((bf16[768,768]{1,0:T(8,128)(2,1)}), bf16[48,768]{1,0:T(8,128)(2,1)}) %reduce-scatter.43.cloned.1.call-update) | async-done | bytes 73744
  1105.8 75.4 %all-reduce.28 = (bf16[768]{0:T(1024)(128)(2,1)S(1)}, bf16[768]{0:T(1024)(128)(2,1)S(1)}, bf16[768]{0:T(1024)(128)(2,1)S(1)}, bf16[768]{0:T(1024)(128)(2,1)S(1)}...) all-reduce(bf16[768]{0:T(1024)(128)(2,1)S(1)} %dynamic-update-slice, ...), channel_id=1, replica_groups=mesh['fsdp'=16,'seq'=2] {'fsdp'}, use_global_device_ids=true, to_apply=%add.13 | all-reduce | flops 13824 | bytes 55296
  1184.7 46.8 %reduce-scatter.45.cloned.1.call-done = bf16[48,768]{1,0:T(8,128)(2,1)} async-done(((bf16[768,768]{1,0:T(8,128)(2,1)}), bf16[48,768]{1,0:T(8,128)(2,1)}) %reduce-scatter.45.cloned.1.call-update) | async-done | bytes 73744
  1233.2 126.4 %reduce-scatter.47.cloned.1.call-done = bf16[48,768]{1,0:T(8,128)(2,1)} async-done(((bf16[768,768]{1,0:T(8,128)(2,1)}), bf16[48,768]{1,0:T(8,128)(2,1)}) %reduce-scatter.47.cloned.1.call-update) | async-done | bytes 73744
  1361.3 126.4 %reduce-scatter.49.cloned.1.call-done = bf16[48,768]{1,0:T(8,128)(2,1)} async-done(((bf16[768,768]{1,0:T(8,128)(2,1)}), bf16[48,768]{1,0:T(8,128)(2,1)}) %reduce-scatter.49.cloned.1.call-update) | async-done | bytes 73744
  1489.4 126.5 %reduce-scatter.51.cloned.1.call-done = bf16[48,768]{1,0:T(8,128)(2,1)} async-done(((bf16[768,768]{1,0:T(8,128)(2,1)}), bf16[48,768]{1,0:T(8,128)(2,1)}) %reduce-scatter.51.cloned.1.call-update) | async-done | bytes 73744
  1617.6 126.3 %reduce-scatter.35.cloned.1.call-done = bf16[48,768]{1,0:T(8,128)(2,1)} async-done(((bf16[768,768]{1,0:T(8,128)(2,1)}), bf16[48,768]{1,0:T(8,128)(2,1)}) %reduce-scatter.35.cloned.1.call-update) | async-done | bytes 73744 | tf_op jit(solution)/shard_map/reduce_scatter | solution.py:460
  1743.9 128.1 %reduce-scatter.33.cloned.1.call-done = bf16[48,768]{1,0:T(8,128)(2,1)} async-done(((bf16[768,768]{1,0:T(8,128)(2,1)}), bf16[48,768]{1,0:T(8,128)(2,1)}) %reduce-scatter.33.cloned.1.call-update) | async-done | bytes 73744 | tf_op jit(solution)/shard_map/reduce_scatter | solution.py:448
  1872.0 128.0 %reduce-scatter.37.cloned.1.call-done = bf16[48,768]{1,0:T(8,128)(2,1)} async-done(((bf16[768,768]{1,0:T(8,128)(2,1)}), bf16[48,768]{1,0:T(8,128)(2,1)}) %reduce-scatter.37.cloned.1.call-update) | async-done | bytes 73744 | tf_op jit(solution)/shard_map/reduce_scatter | solution.py:475
  2000.0 141.7 %reduce-scatter.39.cloned.1.call-done = bf16[48,3072]{1,0:T(8,128)(2,1)} async-done(((bf16[768,3072]{1,0:T(8,128)(2,1)}), bf16[48,3072]{1,0:T(8,128)(2,1)}) %reduce-scatter.39.cloned.1.call-update) | async-done | bytes 294928 | tf_op jit(solution)/shard_map/reduce_scatter | solution.py:487
  2141.6 142.8 %reduce-scatter.41.cloned.1.call-done = bf16[192,768]{1,0:T(8,128)(2,1)} async-done(((bf16[3072,768]{1,0:T(8,128)(2,1)}), bf16[192,768]{1,0:T(8,128)(2,1)}) %reduce-scatter.41.cloned.1.call-update) | async-done | bytes 294928 | tf_op jit(solution)/shard_map/reduce_scatter | solution.py:493
  2303.3 5.8 all-reduce.34.cloned.1.call-done
  (707 shorter events, 406.2 us)
Async XLA Ops:
  7.2 178.4 %copy-start = (bf16[1,512,768]{2,1,0:T(8,128)(2,1)S(1)}, bf16[1,512,768]{2,1,0:T(8,128)(2,1)}, u32[]{:S(2)}) copy-start(bf16[1,512,768]{2,1,0:T(8,128)(2,1)} %param.38) | copy-start | bytes 2359300
  7.2 95.8 %all-gather.19.cloned.1.call-start = ((), (), s32[]{:S(2)}) async-start(), calls=%async_computation.14 | async-start | bytes 1253376 | tf_op jit(solution)/shard_map/all_gather | solution.py:198
  8.0 119.8 %all-gather.23.cloned.1.call-start = ((), (), s32[]{:S(2)}) async-start(), calls=%async_computation.16 | async-start | bytes 1253376 | tf_op jit(solution)/shard_map/all_gather | solution.py:197
  8.7 176.9 %all-gather.27.cloned.1.call-start = ((), (), s32[]{:S(2)}) async-start(), calls=%async_computation.18 | async-start | bytes 1253376 | tf_op jit(solution)/shard_map/all_gather | solution.py:207
  9.4 233.9 %all-gather.31.cloned.1.call-start = ((), (), s32[]{:S(2)}) async-start(), calls=%async_computation.20 | async-start | bytes 1253376 | tf_op jit(solution)/shard_map/all_gather | solution.py:206
  10.0 291.0 %all-gather.21.cloned.1.call-start = ((), (), s32[]{:S(2)}) async-start(), calls=%async_computation.15 | async-start | bytes 1253376 | tf_op jit(solution)/shard_map/all_gather | solution.py:195
  10.6 301.1 %all-gather.39.cloned.1.call-start = ((), (), s32[]{:S(2)}) async-start(), calls=%async_computation.33 | async-start | bytes 2359296 | tf_op jit(solution)/shard_map/all_gather | solution.py:252
  106.3 218.5 %all-gather.41.cloned.1.call-start = ((), (), s32[]{:S(2)}) async-start(), calls=%async_computation.34 | async-start | bytes 2359296 | tf_op jit(solution)/shard_map/all_gather | solution.py:251
  130.7 254.3 %all-gather.25.cloned.1.call-start = ((), (), s32[]{:S(2)}) async-start(), calls=%async_computation.17 | async-start | bytes 1253376 | tf_op jit(solution)/shard_map/all_gather | solution.py:200
  131.5 311.4 %all-gather.29.cloned.1.call-start = ((), (), s32[]{:S(2)}) async-start(), calls=%async_computation.19 | async-start | bytes 1253376 | tf_op jit(solution)/shard_map/all_gather | solution.py:204
  132.2 321.3 %all-gather.43.cloned.1.call-start = ((), (), s32[]{:S(2)}) async-start(), calls=%async_computation.35 | async-start | bytes 2359296 | tf_op jit(solution)/shard_map/all_gather | solution.py:235
  188.6 277.5 %all-gather.45.cloned.1.call-start = ((), (), s32[]{:S(2)}) async-start(), calls=%async_computation.36 | async-start | bytes 2359296 | tf_op jit(solution)/shard_map/all_gather | solution.py:234
  246.3 279.8 %all-gather.33.cloned.1.call-start = ((), (), s32[]{:S(2)}) async-start(), calls=%async_computation.21 | async-start | bytes 1253376 | tf_op jit(solution)/shard_map/all_gather | solution.py:209
  246.9 361.4 %all-gather.35.cloned.1.call-start = ((), (), s32[]{:S(2)}) async-start(), calls=%async_computation.22 | async-start | bytes 5013504 | tf_op jit(solution)/shard_map/all_gather | solution.py:213
  247.6 442.5 %all-gather.37.cloned.1.call-start = ((), (), s32[]{:S(2)}) async-start(), calls=%async_computation.23 | async-start | bytes 5013504 | tf_op jit(solution)/shard_map/all_gather | solution.py:215
  248.2 687.8 %reduce-scatter.25.cloned.1.call-start = ((), (), s32[]{:S(2)}) async-start(), calls=%async_computation.24 | async-start | bytes 2359296 | tf_op jit(solution)/shard_map/reduce_scatter | solution.py:385
  250.7 137.4 %copy-start.47 = (f32[768]{0:T(1024)}, f32[768]{0:T(1024)S(1)}, u32[]{:S(2)}) copy-start(f32[768]{0:T(1024)S(1)} %convert_element_type.412) | copy-start | bytes 9220
  253.1 456.7 %copy-start.59 = (f32[768]{0:T(1024)}, f32[768]{0:T(1024)S(1)}, u32[]{:S(2)}) copy-start(f32[768]{0:T(1024)S(1)} %convert_element_type.424) | copy-start | bytes 9220
  253.2 436.9 %copy-start.69 = (f32[768]{0:T(1024)}, f32[768]{0:T(1024)S(1)}, u32[]{:S(2)}) copy-start(f32[768]{0:T(1024)S(1)} %convert_element_type.425) | copy-start | bytes 9220
  528.8 181.1 %copy-start.53 = (f32[512]{0:T(512)}, f32[512]{0:T(512)S(1)}, u32[]{:S(2)}) copy-start(f32[512]{0:T(512)S(1)} %broadcast_multiply_fusion.7) | copy-start | bytes 6148
  530.3 179.6 %copy-start.63 = (f32[512]{0:T(512)}, f32[512]{0:T(512)S(1)}, u32[]{:S(2)}) copy-start(f32[512]{0:T(512)S(1)} %add_rsqrt_fusion.1) | copy-start | bytes 6148
  530.3 159.8 %copy-start.14 = (f32[512,768]{1,0:T(8,128)S(1)}, f32[512,768]{1,0:T(8,128)}, u32[]{:S(2)}) copy-start(f32[512,768]{1,0:T(8,128)} %copy-done.13) | copy-start | bytes 4718596
  530.3 159.8 %copy-start.71 = (f32[768]{0:T(1024)S(1)}, f32[768]{0:T(1024)}, u32[]{:S(2)}) copy-start(f32[768]{0:T(1024)} %convert_element_type.430) | copy-start | bytes 9220
  716.6 98.1 %copy-start.8 = (f32[512,768]{1,0:T(8,128)S(1)}, f32[512,768]{1,0:T(8,128)}, u32[]{:S(2)}) copy-start(f32[512,768]{1,0:T(8,128)} %copy-done.7) | copy-start | bytes 4718596
  716.6 98.1 %copy-start.48 = (f32[768]{0:T(1024)S(1)}, f32[768]{0:T(1024)}, u32[]{:S(2)}) copy-start(f32[768]{0:T(1024)} %copy-done.47) | copy-start | bytes 9220
  716.6 98.1 %copy-start.50 = (f32[512]{0:T(512)S(1)}, f32[512]{0:T(512)}, u32[]{:S(2)}) copy-start(f32[512]{0:T(512)} %copy-done.49) | copy-start | bytes 6148
  818.9 163.1 %copy-start.5 = (f32[512,768]{1,0:T(8,128)}, f32[512,768]{1,0:T(8,128)S(1)}, u32[]{:S(2)}) copy-start(f32[512,768]{1,0:T(8,128)S(1)} %get-tuple-element.1010) | copy-start | bytes 4718596
  928.1 20.3 reduce-scatter.27.cloned.1.call-start
  928.7 32.1 %reduce-scatter.29.cloned.1.call-start = ((), (), s32[]{:S(2)}) async-start(), calls=%async_computation.26 | async-start | bytes 2359296 | tf_op jit(solution)/shard_map/reduce_scatter | solution.py:351
  929.3 44.0 %reduce-scatter.31.cloned.1.call-start = ((), (), s32[]{:S(2)}) async-start(), calls=%async_computation.27 | async-start | bytes 2359296 | tf_op jit(solution)/shard_map/reduce_scatter | solution.py:354
  929.9 173.7 %reduce-scatter.43.cloned.1.call-start = ((), (), s32[]{:S(2)}) async-start(), calls=%async_computation.37 | async-start | bytes 1253376
  935.4 296.1 %reduce-scatter.45.cloned.1.call-start = ((), (), s32[]{:S(2)}) async-start(), calls=%async_computation.38 | async-start | bytes 1253376
  941.7 417.9 %reduce-scatter.47.cloned.1.call-start = ((), (), s32[]{:S(2)}) async-start(), calls=%async_computation.39 | async-start | bytes 1253376
  954.0 533.7 %reduce-scatter.49.cloned.1.call-start = ((), (), s32[]{:S(2)}) async-start(), calls=%async_computation.40 | async-start | bytes 1253376
  966.4 649.5 %reduce-scatter.51.cloned.1.call-start = ((), (), s32[]{:S(2)}) async-start(), calls=%async_computation.41 | async-start | bytes 1253376
  978.7 765.1 %reduce-scatter.35.cloned.1.call-start = ((), (), s32[]{:S(2)}) async-start(), calls=%async_computation.29 | async-start | bytes 1253376 | tf_op jit(solution)/shard_map/reduce_scatter | solution.py:460
  982.0 890.0 %reduce-scatter.33.cloned.1.call-start = ((), (), s32[]{:S(2)}) async-start(), calls=%async_computation.28 | async-start | bytes 1253376 | tf_op jit(solution)/shard_map/reduce_scatter | solution.py:448
  985.1 1014.9 %reduce-scatter.37.cloned.1.call-start = ((), (), s32[]{:S(2)}) async-start(), calls=%async_computation.30 | async-start | bytes 1253376 | tf_op jit(solution)/shard_map/reduce_scatter | solution.py:475
  988.7 1152.9 %reduce-scatter.39.cloned.1.call-start = ((), (), s32[]{:S(2)}) async-start(), calls=%async_computation.31 | async-start | bytes 5013504 | tf_op jit(solution)/shard_map/reduce_scatter | solution.py:487
  995.3 1289.1 %reduce-scatter.41.cloned.1.call-start = ((), (), s32[]{:S(2)}) async-start(), calls=%async_computation.32 | async-start | bytes 5013504 | tf_op jit(solution)/shard_map/reduce_scatter | solution.py:493
  1003.5 1305.6 %all-reduce.34.cloned.1.call-start = ((), (), s32[]{:S(2)}) async-start(), calls=%async_computation.42 | async-start | bytes 3588096 | tf_op jit(solution)/shard_map/psum | solution.py:532
  1006.8 98.5 %copy-start.19 = (bf16[1,512,768]{1,2,0:T(8,128)(2,1)S(1)}, bf16[1,512,768]{1,2,0:T(8,128)(2,1)}, u32[]{:S(2)}) copy-start(bf16[1,512,768]{1,2,0:T(8,128)(2,1)} %reduce-scatter.27.cloned.1.call-done) | copy-start | bytes 2359300
  1006.8 98.7 %copy-start.27 = (bf16[1,512,768]{1,2,0:T(8,128)(2,1)S(1)}, bf16[1,512,768]{1,2,0:T(8,128)(2,1)}, u32[]{:S(2)}) copy-start(bf16[1,512,768]{1,2,0:T(8,128)(2,1)} %reduce-scatter.31.cloned.1.call-done) | copy-start | bytes 2359300
  1010.3 95.5 %copy-start.68 = (bf16[3072]{0:T(1024)(128)(2,1)S(1)}, bf16[3072]{0:T(1024)(128)(2,1)}, u32[]{:S(2)}) copy-start(bf16[3072]{0:T(1024)(128)(2,1)} %get-tuple-element.1039) | copy-start | bytes 18436
  1184.7 1099.8 %copy-start.4 = (f32[512,768]{1,0:T(8,128)S(1)}, f32[512,768]{1,0:T(8,128)}, u32[]{:S(2)}) copy-start(f32[512,768]{1,0:T(8,128)} %copy-done.3) | copy-start | bytes 4718596
  1184.7 1099.8 %copy-start.44 = (f32[768]{0:T(1024)S(1)}, f32[768]{0:T(1024)}, u32[]{:S(2)}) copy-start(f32[768]{0:T(1024)} %convert_element_type.431) | copy-start | bytes 9220
  1184.7 1099.8 %copy-start.46 = (f32[512]{0:T(512)S(1)}, f32[512]{0:T(512)}, u32[]{:S(2)}) copy-start(f32[512]{0:T(512)} %copy-done.45) | copy-start | bytes 6148
  1184.7 1099.8 %copy-start.52 = (f32[512]{0:T(512)S(1)}, f32[512]{0:T(512)}, u32[]{:S(2)}) copy-start(f32[512]{0:T(512)} %copy-done.51) | copy-start | bytes 6148
  (88 other events, 1347.4 us)
Sparse Core Ops, SparseCore 0:
  10.8 59.0 all-gather.18
  72.7 55.0 all-gather.22
  130.6 54.9 all-gather.26
  188.3 54.9 all-gather.30
  246.0 54.9 all-gather.20
  303.0 8.6 all-gather.38
  313.8 10.9 all-gather.40
  327.6 57.3 all-gather.24
  387.8 54.9 all-gather.28
  444.8 8.6 all-gather.42
  455.1 10.9 all-gather.44
  468.8 57.3 all-gather.32
  528.9 79.3 all-gather.34
  611.0 79.0 all-gather.36
  928.3 7.6 reduce-scatter.24
  938.2 10.2 reduce-scatter.26
  950.6 10.2 reduce-scatter.28
  963.0 10.2 reduce-scatter.30
  978.1 125.4 reduce-scatter.42
  1108.2 123.2 reduce-scatter.44
  1236.3 123.2 reduce-scatter.46
  1364.4 123.2 reduce-scatter.48
  1492.5 123.3 reduce-scatter.50
  1620.5 123.3 reduce-scatter.34
  1748.6 123.3 reduce-scatter.32
  1876.6 123.3 reduce-scatter.36
  2005.0 136.5 reduce-scatter.38
  2147.6 136.7 reduce-scatter.40
  2288.1 20.9 all-reduce.33
where the time goes:
time: 2330 us
  waiting for transfers between devices  1670 us (72%)
  matrix products  255 us (11%)
  blocking collectives  160 us (7%)
  local copies, waits for them, and re-layouts  154 us (7%)
  other arithmetic  67 us (3%)
    unnamed x34, waiting for transfers between devices  527 us
    unnamed x2, blocking collectives  154 us
    reduce_scatter x1, waiting for transfers between devices, body(): lax.psum_scatter(grad_outer_weight.astype(jnp.bfloat16), 'fsdp', scatter_...  143 us
    reduce_scatter x1, waiting for transfers between devices, body(): lax.psum_scatter(grad_inner_weight.astype(jnp.bfloat16), 'fsdp', scatter_...  142 us
    reduce_scatter x1, waiting for transfers between devices, body(): lax.psum_scatter(grad_self_output.astype(jnp.bfloat16), 'fsdp', scatter_d...  128 us
    reduce_scatter x1, waiting for transfers between devices, body(): lax.psum_scatter(grad_cross_output.astype(jnp.bfloat16), 'fsdp', scatter_...  128 us
    reduce_scatter x1, waiting for transfers between devices, body(): lax.psum_scatter(grad_cross_query.astype(jnp.bfloat16), 'fsdp', scatter_d...  126 us
    all_gather x1, waiting for transfers between devices, body(): lax.all_gather(inner_weight, 'fsdp', axis=0, tiled=True)  78 us
  transfers between devices with their start and end apart: 29, of which 28 were waited for; matrix products, arithmetic and copies ran while one was open for 10% of the time, Pallas kernels for 0%

commit v1 on v0

v1 whole, which is shorter than its diff:
```python
import functools
import math
from types import SimpleNamespace
from typing import NamedTuple

import jax
import jax.numpy as jnp
from jax import lax
from jax.experimental import pallas as pl
from jax.experimental.pallas import tpu as pltpu
from jax.sharding import PartitionSpec as P

HEAD_DIM = 64
PAIR = 2 * HEAD_DIM
SEGMENTS = 5
TILE = 256
eps_norm = 1e-05
masked_score = -1e30


class Weights(NamedTuple):
    self_query: jax.Array
    self_query_bias: jax.Array
    self_key: jax.Array
    self_value: jax.Array
    self_value_bias: jax.Array
    self_output: jax.Array
    self_output_bias: jax.Array
    first_gain: jax.Array
    first_shift: jax.Array
    cross_query: jax.Array
    cross_query_bias: jax.Array
    cross_key: jax.Array
    cross_value: jax.Array
    cross_value_bias: jax.Array
    cross_output: jax.Array
    cross_output_bias: jax.Array
    second_gain: jax.Array
    second_shift: jax.Array
    inner_weight: jax.Array
    inner_bias: jax.Array
    outer_weight: jax.Array
    outer_bias: jax.Array
    third_gain: jax.Array
    third_shift: jax.Array


def split_vectors(w):
    return [array for array in w if array.ndim == 1]


def dense(left, right):
    return jnp.dot(left, right, preferred_element_type=jnp.float32)


def dense_back(left, right):
    return lax.dot_general(
        left, right, (((1,), (1,)), ((), ())), preferred_element_type=jnp.float32
    )


def dense_grad(left, right):
    return lax.dot_general(
        left, right, (((0,), (0,)), ((), ())), preferred_element_type=jnp.float32
    )


def column_sum(values):
    return jnp.sum(values, axis=0, dtype=jnp.float32)


def layer_norm(resid, gain, shift):
    center = resid - jnp.mean(resid, axis=-1, keepdims=True)
    spread = jnp.mean(center * center, axis=-1, keepdims=True)
    inverse = lax.rsqrt(spread + eps_norm)
    normed = center * inverse
    return (normed * gain + shift, normed, inverse)


def norm_back(upstream, normed, inverse, gain):
    scaled = upstream * gain
    plain_mean = jnp.mean(scaled, axis=-1, keepdims=True)
    cross_mean = jnp.mean(scaled * normed, axis=-1, keepdims=True)
    result = inverse * (scaled - plain_mean - normed * cross_mean)
    return (result, jnp.sum(upstream * normed, axis=0), jnp.sum(upstream, axis=0))


class Staged:
    staged = True

    def __init__(self):
        self.f = lax.axis_index("fsdp")
        self.c = lax.axis_index("seq")
        self.z, self.y, self.x = self.f // 4, (self.f // 2) % 2, self.f % 2

    def _send(self, array, move):
        pairs = []
        for f in range(16):
            for c in range(2):
                g, d = move(f, c)
                pairs.append((f * 2 + c, g * 2 + d))
        return lax.ppermute(array, ("fsdp", "seq"), pairs)

    def along_z(self, array, k):
        return self._send(array, lambda f, c: ((f + 4 * k) % 16, c))

    def along_x(self, array):
        return self._send(array, lambda f, c: (f ^ 1, c))

    def along_y(self, array):
        return self._send(array, lambda f, c: (f ^ 2, c))

    def along_own(self, array):
        return self._send(array, lambda f, c: (f ^ (1 if c == 0 else 2), c))

    def along_other(self, array):
        return self._send(array, lambda f, c: (f ^ (2 if c == 0 else 1), c))

    def swap(self, array):
        return self._send(array, lambda f, c: (f, 1 - c))


    def _pieces(self, half):
        column = jnp.stack([half] + [self.along_z(half, k) for k in (1, 2, 3)])
        by_x, by_y = self.along_x(column), self.along_y(column)
        by_both = self.along_other(jnp.where(self.c == 0, by_x, by_y))
        return [column, by_x, by_y, by_both]

    def _half(self, array, part):
        width = array.shape[1] // 2
        return lax.dynamic_slice_in_dim(array, part * width, width, 1)

    def gather(self, shards, vectors=None):
        parts = [self._half(s, self.c) for s in shards]
        rows = [p.shape[0] for p in parts]
        width = parts[0].shape[1]
        if vectors is not None:
            flat = jnp.concatenate(vectors)
            parts.append(jnp.pad(flat, (0, 16 * width - flat.shape[0])).reshape(16, width))
        packed = jnp.concatenate(parts) if len(parts) > 1 else parts[0]
        mine = self._pieces(packed)
        theirs = [self.swap(p) for p in mine]
        place = jnp.stack([self.z, self.y * 2 + self.x, self.c]).astype(jnp.int32)
        shapes = [jax.ShapeDtypeStruct((16 * r, 2 * width), packed.dtype) for r in rows]
        out_specs = [
            pl.BlockSpec((4 * r, 2 * width), lambda k, p: (lax.rem(p[0] - k + 4, 4), 0))
            for r in rows
        ]
        if vectors is not None:
            shapes.append(jax.ShapeDtypeStruct((16, 16, width), packed.dtype))
            out_specs.append(
                pl.BlockSpec((4, 16, width), lambda k, p: (lax.rem(p[0] - k + 4, 4), 0, 0))
            )

        def assemble(place_ref, *refs):
            pieces, outs = refs[:8], refs[8:]
            for core in range(2):

                @pl.when(place_ref[2] == core)
                def _():
                    for r in range(4):
                        source = place_ref[1] ^ r
                        for h in range(2):
                            offset = 0
                            columns = slice((core ^ h) * width, (core ^ h) * width + width)
                            for count, out in zip(rows, outs):
                                start = pl.multiple_of(source * count, 16)
                                out[pl.ds(start, count), columns] = pieces[h * 4 + r][
                                    0, offset : offset + count, :
                                ]
                                offset += count
                        if vectors is not None:
                            outs[-1][source] = pieces[r][0, offset : offset + 16, :]

        total = packed.shape[0]
        results = pl.pallas_call(
            assemble,
            out_shape=shapes,
            grid_spec=pltpu.PrefetchScalarGridSpec(
                num_scalar_prefetch=1,
                grid=(4,),
                in_specs=[pl.BlockSpec((1, total, width), lambda k, p: (k, 0, 0))] * 8,
                out_specs=out_specs,
            ),
            compiler_params=pltpu.CompilerParams(vmem_limit_bytes=48 * 2**20),
        )(place, *mine, *theirs)
        if vectors is None:
            return results
        table = results[-1].reshape(16, 16 * width)
        wholes, offset = [], 0
        for v in vectors:
            size = v.shape[0]
            wholes.append(table[:, offset : offset + size].reshape(-1).astype(jnp.float32))
            offset += size
        return results[:-1], wholes


    def _reduce(self, total):
        rows = total.shape[0] // 16
        blocks = total.reshape(4, 2, 2, rows, total.shape[1])
        kind = total.dtype

        def block(y, x):
            return lax.dynamic_slice(
                blocks, (0, y, x, 0, 0), (4, 1, 1, rows, total.shape[1])
            ).reshape(4, rows, total.shape[1])

        y, x = self.y, self.x
        passed = self.along_own(block(1 - y, 1 - x)).astype(jnp.float32)
        first = self.c == 0
        for_x = block(y, 1 - x).astype(jnp.float32) + jnp.where(first, 0.0, passed)
        for_y = block(1 - y, x).astype(jnp.float32) + jnp.where(first, passed, 0.0)
        own = (
            block(y, x).astype(jnp.float32)
            + self.along_x(for_x.astype(kind)).astype(jnp.float32)
            + self.along_y(for_y.astype(kind)).astype(jnp.float32)
        ).astype(kind)

        def at(z):
            return lax.dynamic_index_in_dim(own, z % 4, 0, keepdims=False)

        result = at(self.z).astype(jnp.float32)
        for k in (1, 2, 3):
            result = result + self.along_z(at(self.z + k), k).astype(jnp.float32)
        return result

    def reduce_product(self, left, rights):
        other = jnp.concatenate([self._half(r, 1 - self.c) for r in rights], axis=1)
        own = jnp.concatenate([self._half(r, self.c) for r in rights], axis=1)
        there = self.swap(dense_grad(left, other).astype(jnp.bfloat16))
        total = (dense_grad(left, own) + there.astype(jnp.float32)).astype(jnp.bfloat16)
        mine = self._reduce(total).astype(jnp.bfloat16)
        theirs = self.swap(mine)
        first = self.c == 0
        low = jnp.where(first, mine, theirs).astype(jnp.float32)
        high = jnp.where(first, theirs, mine).astype(jnp.float32)
        results, offset = [], 0
        for r in rights:
            width = r.shape[1] // 2
            results.append(
                jnp.concatenate(
                    [low[:, offset : offset + width], high[:, offset : offset + width]], axis=1
                )
            )
            offset += width
        return results

    def reduce_vectors(self, vectors):
        sizes = [v.shape[0] // 16 for v in vectors]
        table = jnp.concatenate([v.reshape(16, -1) for v in vectors], axis=1)
        used = table.shape[1]
        table = jnp.pad(table, ((0, 0), (0, 1024 - used))).reshape(16 * 8, 128)
        table = table + self.swap(table)
        summed = self._reduce(table).reshape(1024)
        results, offset = [], 0
        for size in sizes:
            results.append(summed[offset : offset + size])
            offset += size
        return results


    def gather_row(self, array):
        return jnp.concatenate([array, self.swap(array)], axis=1)

    def places(self, length):
        steps = jnp.arange(length)
        return jnp.concatenate([self.c * length + steps, (1 - self.c) * length + steps])

    def scatter_row(self, array):
        length = array.shape[1] // 2
        there = self.swap(array[:, length:].astype(jnp.bfloat16))
        return array[:, :length] + there.astype(jnp.float32)


class Plain:
    staged = False

    def gather(self, shards, vectors=None):
        results = [lax.all_gather(s, "fsdp", axis=0, tiled=True) for s in shards]
        if vectors is None:
            return results
        return results, [
            lax.all_gather(v, "fsdp", axis=0, tiled=True).astype(jnp.float32) for v in vectors
        ]

    def _reduce(self, total):
        part = lax.psum_scatter(
            total.astype(jnp.bfloat16), "fsdp", scatter_dimension=0, tiled=True
        )
        return lax.psum(part, "seq").astype(jnp.float32)

    def reduce_product(self, left, rights):
        return [self._reduce(dense_grad(left, r)) for r in rights]

    def reduce_vectors(self, vectors):
        return [self._reduce(v) for v in vectors]

    def gather_row(self, array):
        return lax.all_gather(array, "seq", axis=1, tiled=True)

    def places(self, length):
        return jnp.arange(length * lax.axis_size("seq"))

    def scatter_row(self, array):
        return lax.psum_scatter(
            array.astype(jnp.bfloat16), "seq", scatter_dimension=1, tiled=True
        ).astype(jnp.float32)


def query_marks(ids):
    lanes = jnp.arange(PAIR)[None, :] % HEAD_DIM
    return jnp.where((lanes < SEGMENTS) & (ids[:, None] != lanes), masked_score, 0.0).astype(
        jnp.bfloat16
    )


def key_marks_of(ids):
    lanes = jnp.arange(PAIR)[None, :] % HEAD_DIM
    ones = (lanes >= SEGMENTS) & (lanes < SEGMENTS + 3)
    return (ones | (ids[:, None] == lanes)).astype(jnp.bfloat16)


def against(left, right):
    return lax.dot_general(
        left, right, (((1,), (1,)), ((), ())), preferred_element_type=jnp.float32
    )


def three(value):
    high = value.astype(jnp.bfloat16).astype(jnp.float32)
    rest = value - high
    middle = rest.astype(jnp.bfloat16).astype(jnp.float32)
    return high, middle, rest - middle


def place_three(lanes, base, value, other):
    high, middle, small = three(value)
    first = base + SEGMENTS
    return jnp.where(
        lanes == first,
        high,
        jnp.where(lanes == first + 1, middle, jnp.where(lanes == first + 2, small, other)),
    )


def plan(length, causal, later):
    half = length // 2
    result = []
    for tile in range(2):
        if not causal:
            result.append([(0, 2 * length, False)])
            continue
        ranges = [(0, half, False)] if tile else []
        ranges.append((tile * half, half, True))
        if later:
            ranges.append((length + tile * half, length - tile * half, False))
        result.append(ranges)
    return result


def each_plan(core, length, causal, run):
    if not causal:
        run(plan(length, False, False))
        return
    for later in range(2):
        @pl.when(core == later)
        def _():
            run(plan(length, True, bool(later)))


def forward_kernel(causal, core_ref, q_ref, k_ref, v_ref, qm_ref, km_ref, mixed_ref, qx_ref):
    length = q_ref.shape[0]

    def run(tiles):
        for head in range(2):
            base = HEAD_DIM * (1 - head)

            def own(lanes):
                return (lanes < HEAD_DIM) if head == 0 else (lanes >= HEAD_DIM)

            for tile, ranges in enumerate(tiles):
                rows = slice(tile * TILE, tile * TILE + TILE)
                lanes = lax.broadcasted_iota(jnp.int32, (TILE, PAIR), 1)
                q = jnp.where(own(lanes), q_ref[rows, :], qm_ref[rows, :])
                scores = []
                for start, size, diagonal in ranges:
                    keys = slice(start, start + size)
                    key_lanes = lax.broadcasted_iota(jnp.int32, (size, PAIR), 1)
                    k = jnp.where(own(key_lanes), k_ref[keys, :], km_ref[keys, :])
                    s = against(q, k)
                    if diagonal:
                        i = lax.broadcasted_iota(jnp.int32, s.shape, 0)
                        j = lax.broadcasted_iota(jnp.int32, s.shape, 1)
                        s = jnp.where(j <= i, s, masked_score)
                    scores.append(s)
                highest = functools.reduce(
                    jnp.maximum, [jnp.max(s, axis=1, keepdims=True) for s in scores]
                )
                out = jnp.zeros((TILE, PAIR), jnp.float32)
                for s, (start, size, _) in zip(scores, ranges):
                    keys = slice(start, start + size)
                    key_lanes = lax.broadcasted_iota(jnp.int32, (size, PAIR), 1)
                    v = jnp.where(own(key_lanes), v_ref[keys, :], jnp.ones((), jnp.bfloat16))
                    e = jnp.exp(s - highest).astype(jnp.bfloat16)
                    out = out + jnp.dot(e, v, preferred_element_type=jnp.float32)
                total = pltpu.roll(out, HEAD_DIM, 1)
                mixed = (out / total).astype(jnp.bfloat16)
                if head:
                    mixed = jnp.where(own(lanes), mixed, mixed_ref[rows, :])
                mixed_ref[rows, :] = mixed
                logsum = highest + jnp.log(out)
                qx = place_three(lanes, base, -logsum, q.astype(jnp.float32))
                qx_ref[head, rows, :] = qx.astype(jnp.bfloat16)

    each_plan(core_ref[0], length, causal, run)


def attend(core, query, keys, values, q_marks, k_marks, causal):
    length, width = query.shape
    extent = keys.shape[0]
    pairs = width // PAIR
    column = lambda rows: pl.BlockSpec((rows, PAIR), lambda i, p: (0, i))
    fixed = lambda rows: pl.BlockSpec((rows, PAIR), lambda i, p: (0, 0))
    return pl.pallas_call(
        functools.partial(forward_kernel, causal),
        out_shape=[
            jax.ShapeDtypeStruct((length, width), jnp.bfloat16),
            jax.ShapeDtypeStruct((2 * pairs, length, PAIR), jnp.bfloat16),
        ],
        grid_spec=pltpu.PrefetchScalarGridSpec(
            num_scalar_prefetch=1,
            grid=(pairs,),
            in_specs=[column(length), column(extent), column(extent), fixed(length), fixed(extent)],
            out_specs=[column(length), pl.BlockSpec((2, length, PAIR), lambda i, p: (i, 0, 0))],
        ),
        compiler_params=pltpu.CompilerParams(vmem_limit_bytes=48 * 2**20),
        cost_estimate=pl.CostEstimate(
            flops=16 * length * extent * width, bytes_accessed=8 * extent * width, transcendentals=0
        ),
    )(core, query, keys, values, q_marks, k_marks)


def backward_kernel(
    causal, core_ref, qx_ref, k_ref, v_ref, e_ref, o_ref, km_ref, dq_ref, dk_ref, dv_ref, dk_acc, dv_acc, dq_acc
):
    length = e_ref.shape[0]
    scale = HEAD_DIM ** (-0.5)

    def run(tiles):
        dk_acc[...] = jnp.zeros_like(dk_acc)
        dv_acc[...] = jnp.zeros_like(dv_acc)
        for head in range(2):
            base = HEAD_DIM * (1 - head)

            def own(lanes):
                return (lanes < HEAD_DIM) if head == 0 else (lanes >= HEAD_DIM)

            for tile, ranges in enumerate(tiles):
                rows = slice(tile * TILE, tile * TILE + TILE)
                lanes = lax.broadcasted_iota(jnp.int32, (TILE, PAIR), 1)
                nothing = jnp.zeros((), jnp.bfloat16)
                qx = qx_ref[head, rows, :]
                q = jnp.where(own(lanes), qx, nothing)
                e = jnp.where(own(lanes), e_ref[rows, :], nothing)
                wide = e.astype(jnp.float32)
                delta = jnp.sum(wide * o_ref[rows, :].astype(jnp.float32), axis=1, keepdims=True)
                ex = place_three(lanes, base, -delta, wide).astype(jnp.bfloat16)
                dq = jnp.zeros((HEAD_DIM, TILE), jnp.float32)
                for start, size, diagonal in ranges:
                    keys = slice(start, start + size)
                    key_lanes = lax.broadcasted_iota(jnp.int32, (size, PAIR), 1)
                    k = jnp.where(own(key_lanes), k_ref[keys, :], km_ref[keys, :])
                    v = jnp.where(own(key_lanes), v_ref[keys, :], km_ref[keys, :])
                    p = jnp.exp(against(k, qx))
                    if diagonal:
                        j = lax.broadcasted_iota(jnp.int32, p.shape, 0)
                        i = lax.broadcasted_iota(jnp.int32, p.shape, 1)
                        p = jnp.where(j <= i, p, 0.0)
                    ds = (p * against(v, ex)).astype(jnp.bfloat16)
                    p = p.astype(jnp.bfloat16)
                    dv_acc[keys, :] += jnp.dot(p, e, preferred_element_type=jnp.float32)
                    dk_acc[keys, :] += jnp.dot(ds, q, preferred_element_type=jnp.float32)
                    kt = k_ref[keys, :].T[head * HEAD_DIM : (head + 1) * HEAD_DIM, :]
                    dq = dq + jnp.dot(kt, ds, preferred_element_type=jnp.float32)
                dq_acc[head * HEAD_DIM : (head + 1) * HEAD_DIM, rows] = dq
        dq_ref[...] = (dq_acc[...].T.astype(jnp.bfloat16) * jnp.bfloat16(scale)).astype(jnp.bfloat16)
        dk_ref[...] = dk_acc[...].astype(jnp.bfloat16)
        dv_ref[...] = dv_acc[...].astype(jnp.bfloat16)

    each_plan(core_ref[0], length, causal, run)


def attend_back(core, qx, keys, values, grad, mixed, k_marks, causal):
    length, width = grad.shape
    extent = keys.shape[0]
    pairs = width // PAIR
    column = lambda rows: pl.BlockSpec((rows, PAIR), lambda i, p: (0, i))
    fixed = lambda rows: pl.BlockSpec((rows, PAIR), lambda i, p: (0, 0))
    return pl.pallas_call(
        functools.partial(backward_kernel, causal),
        out_shape=[
            jax.ShapeDtypeStruct((length, width), jnp.bfloat16),
            jax.ShapeDtypeStruct((extent, width), jnp.bfloat16),
            jax.ShapeDtypeStruct((extent, width), jnp.bfloat16),
        ],
        grid_spec=pltpu.PrefetchScalarGridSpec(
            num_scalar_prefetch=1,
            grid=(pairs,),
            in_specs=[
                pl.BlockSpec((2, length, PAIR), lambda i, p: (i, 0, 0)),
                column(extent), column(extent), column(length), column(length), fixed(extent),
            ],
            out_specs=[column(length), column(extent), column(extent)],
            scratch_shapes=[
                pltpu.VMEM((extent, PAIR), jnp.float32),
                pltpu.VMEM((extent, PAIR), jnp.float32),
                pltpu.VMEM((PAIR, length), jnp.float32),
            ],
        ),
        compiler_params=pltpu.CompilerParams(vmem_limit_bytes=48 * 2**20),
        cost_estimate=pl.CostEstimate(
            flops=40 * length * extent * width, bytes_accessed=16 * extent * width, transcendentals=0
        ),
    )(core, qx, keys, values, grad, mixed, k_marks)


def head_slice(array, start, span):
    piece = lax.dynamic_slice_in_dim(array, start, span, 2)
    return piece.reshape(array.shape[0], array.shape[1], 2, span // 2)


def plain_attend(query, keys, values, allowed):
    rows, length, width = query.shape
    span = 2 * HEAD_DIM
    pairs = width // span

    def one_pair(index, carry):
        mixed, logsum = carry
        start = index * span
        query_part = head_slice(query, start, span)
        key_part = head_slice(keys, start, span)
        value_part = head_slice(values, start, span)
        scores = jnp.einsum(
            "rqhe,rkhe->rhqk", query_part, key_part, preferred_element_type=jnp.float32
        )
        scores = jnp.where(allowed[:, None], scores, masked_score)
        highest = jnp.max(scores, axis=-1, keepdims=True)
        exponent = jnp.exp(scores - highest)
        total = jnp.sum(exponent, axis=-1, keepdims=True)
        probs = (exponent / total).astype(jnp.bfloat16)
        part = jnp.einsum("rhqk,rkhe->rqhe", probs, value_part, preferred_element_type=jnp.float32)
        mixed = lax.dynamic_update_slice_in_dim(mixed, part.reshape(rows, length, span), start, 2)
        logsum = lax.dynamic_update_slice_in_dim(
            logsum, (highest + jnp.log(total))[None, :, :, :, 0], index, 0
        )
        return (mixed, logsum)

    mixed = jnp.zeros((rows, length, width), jnp.float32)
    logsum = jnp.zeros((pairs, rows, 2, length), jnp.float32)
    return lax.fori_loop(0, pairs, one_pair, (mixed, logsum))


def plain_attend_back(query, keys, values, allowed, logsum, grad_mixed):
    rows, length, width = query.shape
    extent = keys.shape[1]
    span = 2 * HEAD_DIM
    pairs = width // span

    def one_pair(index, carry):
        start = index * span
        query_part = head_slice(query, start, span)
        key_part = head_slice(keys, start, span)
        value_part = head_slice(values, start, span)
        grad_part = head_slice(grad_mixed, start, span)
        scores = jnp.einsum(
            "rqhe,rkhe->rhqk", query_part, key_part, preferred_element_type=jnp.float32
        )
        scores = jnp.where(allowed[:, None], scores, masked_score)
        pair_logsum = lax.dynamic_index_in_dim(logsum, index, 0, keepdims=False)
        probs = jnp.exp(scores - pair_logsum[..., None])
        prob_grad = jnp.einsum(
            "rqhe,rkhe->rhqk", grad_part, value_part, preferred_element_type=jnp.float32
        )
        row_total = jnp.sum(probs * prob_grad, axis=-1, keepdims=True)
        score_grad = (probs * (prob_grad - row_total)).astype(jnp.bfloat16)
        query_grad = jnp.einsum(
            "rhqk,rkhe->rqhe", score_grad, key_part, preferred_element_type=jnp.float32
        )
        grad_query = lax.dynamic_update_slice_in_dim(
            carry[0], query_grad.reshape(rows, length, span), start, 2
        )
        probs_low = probs.astype(jnp.bfloat16)
        value_grad = jnp.einsum(
            "rhqk,rqhe->rkhe", probs_low, grad_part, preferred_element_type=jnp.float32
        )
        key_grad = jnp.einsum(
            "rhqk,rqhe->rkhe", score_grad, query_part, preferred_element_type=jnp.float32
        )
        grad_keys = lax.dynamic_update_slice_in_dim(
            carry[1], key_grad.reshape(rows, extent, span), start, 2
        )
        grad_values = lax.dynamic_update_slice_in_dim(
            carry[2], value_grad.reshape(rows, extent, span), start, 2
        )
        return (grad_query, grad_keys, grad_values)

    start_query = jnp.zeros((rows, length, width), jnp.float32)
    start_keys = jnp.zeros((rows, extent, width), jnp.float32)
    return lax.fori_loop(0, pairs, one_pair, (start_query, start_keys, start_keys))


def attention(net, query, keys, values, target_ids, key_ids, causal):
    rows, length, width = query.shape
    if net.staged and rows == 1 and length == 2 * TILE:
        core = net.c.reshape(1)
        k_marks = key_marks_of(key_ids[0])
        q_marks = query_marks(target_ids[0])
        mixed, qx = attend(core, query[0], keys[0], values[0], q_marks, k_marks, causal)

        def back(grad):
            results = attend_back(core, qx, keys[0], values[0], grad, mixed, k_marks, causal)
            return [array[None] for array in results]

        return mixed, back
    allowed = target_ids[:, :, None] == key_ids[:, None, :]
    if causal:
        query_places = lax.axis_index("seq") * length + jnp.arange(length)
        allowed &= net.places(length)[None, None, :] <= query_places[None, :, None]
    mixed, logsum = plain_attend(query, keys, values, allowed)

    def plain_back(grad):
        query_sum, key_sum, value_sum = plain_attend_back(
            query, keys, values, allowed, logsum, grad.reshape(rows, length, width)
        )
        return [query_sum.astype(jnp.bfloat16) * HEAD_DIM ** (-0.5), key_sum, value_sum]

    return mixed.astype(jnp.bfloat16).reshape(rows * length, width), plain_back


def body(staged, hidden_in, memory, target_ids, memory_ids, out_grad, *weights):
    w = Weights(*weights)
    net = Staged() if staged else Plain()
    all_ = SimpleNamespace()
    (all_.self_query, all_.self_key, all_.self_value), vectors = net.gather(
        [w.self_query, w.self_key, w.self_value], split_vectors(w)
    )
    (
        self_query_bias, self_value_bias, self_output_bias, first_gain, first_shift,
        cross_query_bias, cross_value_bias, cross_output_bias, second_gain, second_shift,
        inner_bias, outer_bias, third_gain, third_shift,
    ) = vectors
    all_.cross_key, all_.cross_value, all_.self_output = net.gather(
        [w.cross_key, w.cross_value, w.self_output]
    )
    all_.cross_query, all_.cross_output = net.gather([w.cross_query, w.cross_output])
    (all_.inner_weight,) = net.gather([w.inner_weight])
    (all_.outer_weight,) = net.gather([w.outer_weight])

    rows, length, width = hidden_in.shape
    tokens = rows * length
    scale = HEAD_DIM ** (-0.5)
    flat_in = hidden_in.reshape(tokens, width)
    flat_memory = memory.reshape(tokens, width)

    def flat(array):
        return array.astype(jnp.bfloat16).reshape(tokens, width)

    def low(array):
        return array.astype(jnp.bfloat16).reshape(rows, length, width)

    row_ids, source_ids = net.gather_row(target_ids), net.gather_row(memory_ids)
    key_one = low(dense(flat_in, all_.self_key))
    value_one = low(dense(flat_in, all_.self_value) + self_value_bias)
    query_one = low((dense(flat_in, all_.self_query) + self_query_bias) * scale)
    keys_one, values_one = net.gather_row(key_one), net.gather_row(value_one)
    mixed_one, back_one = attention(
        net, query_one, keys_one, values_one, target_ids, row_ids, True
    )

    key_two = low(dense(flat_memory, all_.cross_key))
    value_two = low(dense(flat_memory, all_.cross_value) + cross_value_bias)
    keys_two, values_two = net.gather_row(key_two), net.gather_row(value_two)

    resid_one = (
        flat_in.astype(jnp.float32) + dense(mixed_one, all_.self_output) + self_output_bias
    )
    first, normed_one, inverse_one = layer_norm(resid_one, first_gain, first_shift)
    first = first.astype(jnp.bfloat16)
    query_two = low((dense(first, all_.cross_query) + cross_query_bias) * scale)
    mixed_two, back_two = attention(
        net, query_two, keys_two, values_two, target_ids, source_ids, False
    )
    resid_two = (
        first.astype(jnp.float32) + dense(mixed_two, all_.cross_output) + cross_output_bias
    )
    second, normed_two, inverse_two = layer_norm(resid_two, second_gain, second_shift)
    second = second.astype(jnp.bfloat16)
    inner = dense(second, all_.inner_weight) + inner_bias
    cumulative = 0.5 * (1.0 + lax.erf(inner * math.sqrt(0.5)))
    active = (inner * cumulative).astype(jnp.bfloat16)
    density = jnp.exp(-0.5 * inner * inner) * (1.0 / math.sqrt(2.0 * math.pi))
    slope = cumulative + inner * density
    resid_three = second.astype(jnp.float32) + dense(active, all_.outer_weight) + outer_bias
    final, normed_three, inverse_three = layer_norm(resid_three, third_gain, third_shift)
    layer_out = final.astype(jnp.bfloat16).reshape(rows, length, width)

    g, sums = SimpleNamespace(), SimpleNamespace()
    keep = (target_ids > 0).astype(jnp.float32).reshape(tokens, 1)
    upstream = out_grad.reshape(tokens, width).astype(jnp.float32) * keep
    grad_three, sums.third_gain, sums.third_shift = norm_back(
        upstream, normed_three, inverse_three, third_gain
    )
    grad_outer = grad_three.astype(jnp.bfloat16)
    sums.outer_bias = column_sum(grad_outer)
    (g.outer_weight,) = net.reduce_product(active, [grad_outer])
    grad_active = dense_back(grad_outer, all_.outer_weight)
    grad_inner = (grad_active * slope).astype(jnp.bfloat16)
    sums.inner_bias = column_sum(grad_inner)
    (g.inner_weight,) = net.reduce_product(second, [grad_inner])
    grad_second = grad_three + dense_back(grad_inner, all_.inner_weight)
    grad_two, sums.second_gain, sums.second_shift = norm_back(
        grad_second, normed_two, inverse_two, second_gain
    )
    branch_two = grad_two.astype(jnp.bfloat16)
    sums.cross_output_bias = column_sum(branch_two)
    (g.cross_output,) = net.reduce_product(mixed_two, [branch_two])
    query_grad_two, key_sum_two, value_sum_two = back_two(
        flat(dense_back(branch_two, all_.cross_output))
    )
    key_grad_two = flat(net.scatter_row(key_sum_two))
    value_grad_two = flat(net.scatter_row(value_sum_two))
    query_grad_two = flat(query_grad_two)
    sums.cross_query_bias = column_sum(query_grad_two)
    sums.cross_value_bias = column_sum(value_grad_two)
    (g.cross_query,) = net.reduce_product(first, [query_grad_two])
    g.cross_key, g.cross_value = net.reduce_product(flat_memory, [key_grad_two, value_grad_two])
    memory_grad = low(
        dense_back(key_grad_two, all_.cross_key) + dense_back(value_grad_two, all_.cross_value)
    )
    grad_first = grad_two + dense_back(query_grad_two, all_.cross_query)
    grad_one, sums.first_gain, sums.first_shift = norm_back(
        grad_first, normed_one, inverse_one, first_gain
    )
    branch_one = grad_one.astype(jnp.bfloat16)
    sums.self_output_bias = column_sum(branch_one)
    (g.self_output,) = net.reduce_product(mixed_one, [branch_one])
    query_grad_one, key_sum_one, value_sum_one = back_one(
        flat(dense_back(branch_one, all_.self_output))
    )
    key_grad_one = flat(net.scatter_row(key_sum_one))
    value_grad_one = flat(net.scatter_row(value_sum_one))
    query_grad_one = flat(query_grad_one)
    sums.self_query_bias = column_sum(query_grad_one)
    sums.self_value_bias = column_sum(value_grad_one)
    g.self_query, g.self_key, g.self_value = net.reduce_product(
        flat_in, [query_grad_one, key_grad_one, value_grad_one]
    )
    input_grad = low(
        grad_one
        + dense_back(query_grad_one, all_.self_query)
        + dense_back(key_grad_one, all_.self_key)
        + dense_back(value_grad_one, all_.self_value)
    )
    (
        g.self_query_bias, g.self_value_bias, g.self_output_bias, g.first_gain, g.first_shift,
        g.cross_query_bias, g.cross_value_bias, g.cross_output_bias, g.second_gain,
        g.second_shift, g.inner_bias, g.outer_bias, g.third_gain, g.third_shift,
    ) = net.reduce_vectors(
        [
            sums.self_query_bias, sums.self_value_bias, sums.self_output_bias, sums.first_gain,
            sums.first_shift, sums.cross_query_bias, sums.cross_value_bias,
            sums.cross_output_bias, sums.second_gain, sums.second_shift, sums.inner_bias,
            sums.outer_bias, sums.third_gain, sums.third_shift,
        ]
    )
    return (layer_out, input_grad, memory_grad, *Weights(**vars(g)))


def solution(mesh):
    staged = mesh.shape["fsdp"] == 16 and mesh.shape["seq"] == 2
    row, ids = P("fsdp", "seq", None), P("fsdp", "seq")
    matrix, vector = P("fsdp", None), P("fsdp")
    weights = Weights(
        matrix, vector, matrix, matrix, vector, matrix, vector, vector, vector, matrix, vector,
        matrix, matrix, vector, matrix, vector, vector, vector, matrix, vector, matrix, vector,
        vector, vector,
    )
    return jax.shard_map(
        functools.partial(body, staged),
        mesh=mesh,
        in_specs=(row, row, ids, ids, row, *weights),
        out_specs=(row, row, row, *weights),
        check_vma=False,
    )
```

time: 2330 us -> 531 us (0.23)
  waiting for transfers between devices: 1670 us -> 140 us
  matrix products: 255 us -> 72.8 us
  blocking collectives: 160 us -> 0 us
  starting transfers between devices: 1.16 us -> 130 us
  local copies, waits for them, and re-layouts: 154 us -> 60 us
  Pallas kernels: 0 us -> 74.8 us
    reduce_scatter x9 -> x0, waiting for transfers between devices: 688 us -> none  [the longest x1 143 us: body(): lax.psum_scatter(grad_outer_weight.astype(jnp.bfloat16), 'fsdp', scatter_...]
    unnamed x34 -> x0, waiting for transfers between devices: 527 us -> none
    all_gather x14 -> x0, waiting for transfers between devices: 448 us -> none  [the longest x1 78 us: body(): lax.all_gather(inner_weight, 'fsdp', axis=0, tiled=True)]
    unnamed x2 -> x0, blocking collectives: 154 us -> none
    ppermute x0 -> x123, waiting for transfers between devices: none -> 140 us  [_send(): return lax.ppermute(array, ('fsdp', 'seq'), pairs)]
    dot_general x84 -> x0, matrix products: 139 us -> none  [the longest x12 47.8 us: one_pair(): jnp.einsum('rqhe,rkhe->rhqk', grad_part, value_part, preferred_element_ty...]
    ppermute x0 -> x123, starting transfers between devices: none -> 130 us  [_send(): return lax.ppermute(array, ('fsdp', 'seq'), pairs)]
    pallas_call x0 -> x9, Pallas kernels: none -> 74.8 us  [the longest x2 33.1 us: attend_back(): pl.pallas_call(functools.partial(backward_kernel, causal), out_shape=[jax...]
  transfers between devices with their start and end apart: 29 -> 123, of which waited for: 28 -> 39; matrix products, arithmetic and copies ran while one was open for 10% -> 21% of each run, Pallas kernels for 0% -> 5%
where the time goes in v1:
time: 531 us; the launch traced here: 524 us
  waiting for transfers between devices  140 us (26%)
  starting transfers between devices  130 us (24%)
  Pallas kernels  74.8 us (14%)
  matrix products  72.8 us (14%)
  local copies, waits for them, and re-layouts  60 us (11%)
  other arithmetic  43.7 us (8%)
    ppermute x123, waiting for transfers between devices, _send(): return lax.ppermute(array, ('fsdp', 'seq'), pairs)  140 us
    ppermute x123, starting transfers between devices, _send(): return lax.ppermute(array, ('fsdp', 'seq'), pairs)  130 us
    pallas_call x2, Pallas kernels, attend_back(): pl.pallas_call(functools.partial(backward_kernel, causal), out_shape=[jax...  33.1 us
    dot_general x10, matrix products, dense_back(): lax.dot_general(left, right, (((1,), (1,)), ((), ())), preferred_element_...  26.8 us
    pallas_call x2, Pallas kernels, attend(): pl.pallas_call(functools.partial(forward_kernel, causal), out_shape=[jax....  25.1 us
    dot_general x10, matrix products, dense(): return jnp.dot(left, right, preferred_element_type=jnp.float32)  24 us
    dot_general x14, matrix products, dense_grad(): lax.dot_general(left, right, (((0,), (0,)), ((), ())), preferred_element_...  22.1 us
    pallas_call x5, Pallas kernels, gather(): pl.pallas_call(assemble, out_shape=shapes, grid_spec=pltpu.PrefetchScalar...  16.6 us
  transfers between devices with their start and end apart: 123, of which 39 were waited for; matrix products, arithmetic and copies ran while one was open for 21% of the time, Pallas kernels for 5%

profile of v1, /device:TPU:0, one launch (start us, length us, event | category | flops | bytes accessed | tf_op | source)
XLA Modules:
  0.0 524.0 jit_solution(16200717581680451983)
XLA Ops:
  0.8 9.5 %concatenate.90 = bf16[816]{0:T(1024)(128)(2,1)S(1)} concatenate(bf16[48]{0:T(256)(128)(2,1)} %param.35, bf16[48]{0:T(256)(128)(2,1)} %param.38, bf16[48]{0:T(256)(128)(2,1)} %param.40, bf16[48]{0:T(256)(128)(2,1)} %param.41, bf16[48]{0:T(256)(128)(2,1)} %param.42, bf16[48]{0:T(256)(128)(2,1)} %param.44, bf16[48]{0:T(256)(128)(2,1)} %param.47, bf16[48]{0:T(256)(128)(2,1)} %param.49, ...), dimensions={0} | concatenate | bytes 3264 | tf_op jit(solution)/shard_map/concatenate | solution.py:138
  12.7 5.1 collective-permute-start.2
  29.5 3.3 collective-permute-done.24
  32.8 5.6 %collective-permute-start.13 = (bf16[144,384]{1,0:T(8,128)(2,1)S(1)}, bf16[144,384]{1,0:T(8,128)(2,1)S(1)}, u32[]{:S(2)}, u32[]{:S(2)}) collective-permute-start(bf16[144,384]{1,0:T(8,128)(2,1)S(1)} %get-tuple-element.169), channel_id=1, source_target_pairs={{0,8},{1,9},{2,10},{3,11},{4,12},{5,13},{6,14},{7,15},{8,16},{9,17... | collective-permute-start | bytes 331784 | tf_op jit(solution)/shard_map/ppermute | solution.py:102
  39.2 3.4 collective-permute-start
  42.6 5.9 %collective-permute-start.37 = (bf16[48,1536]{1,0:T(8,128)(2,1)S(1)}, bf16[48,1536]{1,0:T(8,128)(2,1)S(1)}, u32[]{:S(2)}, u32[]{:S(2)}) collective-permute-start(bf16[48,1536]{1,0:T(8,128)(2,1)S(1)} %constant_dynamic-slice_fusion.11), channel_id=1, source_target_pairs={{0,16},{1,17},{2,18},{3,19},{4,20},{5,21},{6,22},{7,23},{8,24},{9,... | collective-permute-start | bytes 442376 | tf_op jit(solution)/shard_map/ppermute | solution.py:102
  48.8 3.5 collective-permute-start.48
  52.6 7.1 %collective-permute-start.16 = (bf16[4,144,384]{2,1,0:T(8,128)(2,1)S(1)}, bf16[4,144,384]{2,1,0:T(8,128)(2,1)S(1)}, u32[]{:S(2)}, u32[]{:S(2)}) collective-permute-start(bf16[4,144,384]{2,1,0:T(8,128)(2,1)S(1)} %pad_maximum_fusion.3.refs_0_), channel_id=1, source_target_pairs={{0,2},{1,3},{2,0},{3,1},{4,6},{5,7},{6,4},{7,5},{8,10},{9,11},{10,... | collective-permute-start | bytes 1327112 | tf_op jit(solution)/shard_map/ppermute | solution.py:102
  70.1 4.9 collective-permute-done.46
  80.1 7.9 %collective-permute-done.17.refs_2_ = bf16[4,144,384]{2,1,0:T(8,128)(2,1)S(1)} collective-permute-done((bf16[4,144,384]{2,1,0:T(8,128)(2,1)S(1)}, bf16[4,144,384]{2,1,0:T(8,128)(2,1)S(1)}, u32[]{:S(2)}, u32[]{:S(2)}) %collective-permute-start.17) | collective-permute-done | bytes 442400 | tf_op jit(solution)/shard_map/ppermute | solution.py:102
  92.3 6.3 %collective-permute-done.4.refs_2_ = bf16[4,160,384]{2,1,0:T(8,128)(2,1)S(1)} collective-permute-done((bf16[4,160,384]{2,1,0:T(8,128)(2,1)S(1)}, bf16[4,160,384]{2,1,0:T(8,128)(2,1)S(1)}, u32[]{:S(2)}, u32[]{:S(2)}) %collective-permute-start.4) | collective-permute-done | bytes 491552 | tf_op jit(solution)/shard_map/ppermute | solution.py:102
  99.6 5.3 %collective-permute-done.28.refs_3_ = bf16[4,96,384]{2,1,0:T(8,128)(2,1)S(1)} collective-permute-done((bf16[4,96,384]{2,1,0:T(8,128)(2,1)S(1)}, bf16[4,96,384]{2,1,0:T(8,128)(2,1)S(1)}, u32[]{:S(2)}, u32[]{:S(2)}) %collective-permute-start.28) | collective-permute-done | bytes 294944 | tf_op jit(solution)/shard_map/ppermute | solution.py:102
  108.2 9.5 %collective-permute-done.40.refs_2_ = bf16[4,48,1536]{2,1,0:T(8,128)(2,1)} collective-permute-done((bf16[4,48,1536]{2,1,0:T(8,128)(2,1)S(1)}, bf16[4,48,1536]{2,1,0:T(8,128)(2,1)}, u32[]{:S(2)}, u32[]{:S(2)}) %collective-permute-start.40) | collective-permute-done | bytes 589856 | tf_op jit(solution)/shard_map/ppermute | solution.py:102
  120.4 5.3 %collective-permute-done.50.refs_2_ = bf16[4,192,384]{2,1,0:T(8,128)(2,1)} collective-permute-done((bf16[4,192,384]{2,1,0:T(8,128)(2,1)S(1)}, bf16[4,192,384]{2,1,0:T(8,128)(2,1)}, u32[]{:S(2)}, u32[]{:S(2)}) %collective-permute-start.50) | collective-permute-done | bytes 589856 | tf_op jit(solution)/shard_map/ppermute | solution.py:102
  126.2 4.1 collective-permute-done.18.refs_3_
  132.2 7.0 %collective-permute-done.5.refs_3_ = bf16[4,160,384]{2,1,0:T(8,128)(2,1)S(1)} collective-permute-done((bf16[4,160,384]{2,1,0:T(8,128)(2,1)S(1)}, bf16[4,160,384]{2,1,0:T(8,128)(2,1)S(1)}, u32[]{:S(2)}, u32[]{:S(2)}) %collective-permute-start.5) | collective-permute-done | bytes 491552 | tf_op jit(solution)/shard_map/ppermute | solution.py:102
  157.5 3.2 fusion.28
  160.9 3.2 fusion.25
  166.8 3.1 fusion.26
  170.9 5.2 shard_map.489
  176.2 5.3 %shard_map.490 = bf16[3072,768]{1,0:T(8,128)(2,1)} custom-call(s32[3]{0:T(128)S(1)} %pad_add_fusion.2.place_ref, bf16[4,192,384]{2,1,0:T(8,128)(2,1)S(1)} %pad_maximum_fusion.1.refs_0_, bf16[4,192,384]{2,1,0:T(8,128)(2,1)S(1)} %collective-permute-done.49.refs_1_, bf16[4,192,384]{2,1,0:T(8,128)(2,1)} %collective-permute-done.50.refs_2_, ...), custom_call_target="tpu_custom_call" | custom-call | tf_op jit(solution)/shard_map/pallas_call | solution.py:176
  186.9 10.4 %shard_map.485 = (bf16[512,768]{1,0:T(8,128)(2,1)S(1)}, bf16[12,512,128]{2,1,0:T(8,128)(2,1)S(1)}) custom-call(s32[1]{0:T(128)} %bitcast.1.core_ref, bf16[512,768]{1,0:T(8,128)(2,1)S(1)} %fusion.24.q_ref, bf16[1024,768]{1,0:T(8,128)(2,1)S(1)} %maximum_bitcast_fusion.k_ref, bf16[1024,768]{1,0:T(8,128)(2,1)} %maximum_bitcast_fusion.1.v_ref, ...), custom_call_target="tpu_custom_call" | custom-call | flops 6442450944 | bytes 6291456 | tf_op jit(solution)/shard_map/pallas_call | solution.py:424
  203.4 14.7 %shard_map.488 = (bf16[512,768]{1,0:T(8,128)(2,1)S(1)}, bf16[12,512,128]{2,1,0:T(8,128)(2,1)S(1)}) custom-call(s32[1]{0:T(128)} %bitcast.1.core_ref, bf16[512,768]{1,0:T(8,128)(2,1)S(1)} %multiply_convert_fusion.1.q_ref, bf16[1024,768]{1,0:T(8,128)(2,1)S(1)} %maximum_bitcast_fusion.2.k_ref, bf16[1024,768]{1,0:T(8,128)(2,1)} %maximum_bitcast_fusion.3.v_ref, ...), custom_call_target="tpu_custom_call" | custom-call | flops 6442450944 | bytes 6291456 | tf_op jit(solution)/shard_map/pallas_call | solution.py:424
  219.9 6.8 %multiply_convert_fusion = (bf16[512,3072]{1,0:T(8,128)(2,1)S(1)}, f32[512,3072]{1,0:T(8,128)}) fusion(f32[3072]{0:T(1024)S(1)} %reshape.559, bf16[512,768]{1,0:T(8,128)(2,1)S(1)} %add_convert_fusion.10, bf16[768,3072]{1,0:T(8,128)(2,1)} %shard_map.489), kind=kOutput, calls=%fused_computation.8 | convolution fusion | flops 2425356288 | bytes 14954496 | tf_op jit(solution)/shard_map/dot_general | solution.py:53
  234.3 7.4 %convert_reduce_fusion = (f32[3072]{0:T(1024)}, bf16[512,3072]{1,0:T(8,128)(2,1)S(1)}) fusion(f32[512,3072]{1,0:T(8,128)} %get-tuple-element.203, f32[3072]{0:T(1024)S(1)} %reshape.559, bf16[512,768]{1,0:T(8,128)(2,1)S(1)} %get-tuple-element.78, bf16[3072,768]{1,0:T(8,128)(2,1)S(1)} %bitcast.424), kind=kOutput, calls=%fused_computation.7 | convolution fusion | flops 2436363264 | bytes 14966784 | tf_op jit(solution)/shard_map/dot_general | solution.py:57
  241.7 3.9 multiply_reduce_fusion
  247.1 19.6 %shard_map.491 = (bf16[512,768]{1,0:T(8,128)(2,1)S(1)}, bf16[1024,768]{1,0:T(8,128)(2,1)S(1)}, bf16[1024,768]{1,0:T(8,128)(2,1)S(1)}) custom-call(s32[1]{0:T(128)} %bitcast.1.core_ref, bf16[12,512,128]{2,1,0:T(8,128)(2,1)} %copy-done.51, bf16[1024,768]{1,0:T(8,128)(2,1)} %copy-done.6, bf16[1024,768]{1,0:T(8,128)(2,1)} %maximum_bitcast_fusion.3.v_ref, ...), custom_call_target="tpu_custom_call" | custom-call | flops 16106127360 | bytes 12582912 | tf_op jit(solution)/shard_map/pallas_call | solution.py:499
  274.2 3.3 convolution_convert_fusion
  277.5 13.5 %shard_map.492 = (bf16[512,768]{1,0:T(8,128)(2,1)S(1)}, bf16[1024,768]{1,0:T(8,128)(2,1)S(1)}, bf16[1024,768]{1,0:T(8,128)(2,1)S(1)}) custom-call(s32[1]{0:T(128)} %bitcast.1.core_ref, bf16[12,512,128]{2,1,0:T(8,128)(2,1)} %copy-done.50, bf16[1024,768]{1,0:T(8,128)(2,1)} %copy-done.5, bf16[1024,768]{1,0:T(8,128)(2,1)} %maximum_bitcast_fusion.1.v_ref, ...), custom_call_target="tpu_custom_call" | custom-call | flops 16106127360 | bytes 12582912 | tf_op jit(solution)/shard_map/pallas_call | solution.py:499
  292.0 9.2 %collective-permute-start.56 = (bf16[1,512,768]{2,1,0:T(8,128)(2,1)}, bf16[1,512,768]{2,1,0:T(8,128)(2,1)}, u32[]{:S(2)}, u32[]{:S(2)}) collective-permute-start(bf16[1,512,768]{2,1,0:T(8,128)(2,1)} %slice.199), channel_id=1, source_target_pairs={{0,1},{1,0},{2,3},{3,2},{4,5},{5,4},{6,7},{7,6},{8,9},{9,8},{10,11... | collective-permute-start | bytes 2359304 | tf_op jit(solution)/shard_map/ppermute | solution.py:102
  322.6 3.4 fusion.194
  331.6 3.9 collective-permute-done.76
  336.8 3.8 collective-permute-done.84
  341.9 3.8 collective-permute-done.100
  369.7 4.1 fusion.61
  401.1 3.0 collective-permute-start.89
  405.7 4.2 collective-permute-start.105
  411.6 3.1 collective-permute-done.104
  423.5 5.0 collective-permute-done.92
  430.7 3.3 add_convert_fusion.1
  438.5 4.2 collective-permute-start.97
  444.7 3.3 collective-permute-done.96
  451.7 5.8 %collective-permute-done.61 = bf16[4,48,1152]{2,1,0:T(8,128)(2,1)S(1)} collective-permute-done((bf16[4,48,1152]{2,1,0:T(8,128)(2,1)S(1)}, bf16[4,48,1152]{2,1,0:T(8,128)(2,1)S(1)}, u32[]{:S(2)}, u32[]{:S(2)}) %collective-permute-start.61) | collective-permute-done | bytes 442400 | tf_op jit(solution)/shard_map/ppermute | solution.py:102
  463.8 7.0 %collective-permute-done.63 = bf16[4,48,1152]{2,1,0:T(8,128)(2,1)S(1)} collective-permute-done((bf16[4,48,1152]{2,1,0:T(8,128)(2,1)S(1)}, bf16[4,48,1152]{2,1,0:T(8,128)(2,1)S(1)}, u32[]{:S(2)}, u32[]{:S(2)}) %collective-permute-start.63) | collective-permute-done | bytes 442400 | tf_op jit(solution)/shard_map/ppermute | solution.py:102
  474.2 9.3 %collective-permute-done.110 = bf16[4,48,1536]{2,1,0:T(8,128)(2,1)S(1)} collective-permute-done((bf16[4,48,1536]{2,1,0:T(8,128)(2,1)S(1)}, bf16[4,48,1536]{2,1,0:T(8,128)(2,1)S(1)}, u32[]{:S(2)}, u32[]{:S(2)}) %collective-permute-start.110) | collective-permute-done | bytes 589856 | tf_op jit(solution)/shard_map/ppermute | solution.py:102
  486.4 8.3 %collective-permute-done.118 = bf16[4,192,384]{2,1,0:T(8,128)(2,1)S(1)} collective-permute-done((bf16[4,192,384]{2,1,0:T(8,128)(2,1)S(1)}, bf16[4,192,384]{2,1,0:T(8,128)(2,1)S(1)}, u32[]{:S(2)}, u32[]{:S(2)}) %collective-permute-start.118) | collective-permute-done | bytes 589856 | tf_op jit(solution)/shard_map/ppermute | solution.py:102
  505.8 10.7 %collective-permute-done.112 = bf16[48,1536]{1,0:T(8,128)(2,1)S(1)} collective-permute-done((bf16[48,1536]{1,0:T(8,128)(2,1)S(1)}, bf16[48,1536]{1,0:T(8,128)(2,1)S(1)}, u32[]{:S(2)}, u32[]{:S(2)}) %collective-permute-start.112) | collective-permute-done | bytes 147488 | tf_op jit(solution)/shard_map/ppermute | solution.py:102
  516.7 4.8 collective-permute-done.120
  (649 shorter events, 227.9 us)
Async XLA Ops:
  12.7 35.8 %collective-permute-start.2 = (bf16[160,384]{1,0:T(8,128)(2,1)S(1)}, bf16[160,384]{1,0:T(8,128)(2,1)S(1)}, u32[]{:S(2)}, u32[]{:S(2)}) collective-permute-start(bf16[160,384]{1,0:T(8,128)(2,1)S(1)} %get-tuple-element.167), channel_id=1, source_target_pairs={{0,24},{1,25},{2,26},{3,27},{4,28},{5,29},{6,30},{7,31},{8,0},{9,1... | collective-permute-start | bytes 368648 | tf_op jit(solution)/shard_map/ppermute | solution.py:102
  17.8 31.0 %collective-permute-start.1 = (bf16[160,384]{1,0:T(8,128)(2,1)S(1)}, bf16[160,384]{1,0:T(8,128)(2,1)S(1)}, u32[]{:S(2)}, u32[]{:S(2)}) collective-permute-start(bf16[160,384]{1,0:T(8,128)(2,1)S(1)} %get-tuple-element.167), channel_id=1, source_target_pairs={{0,16},{1,17},{2,18},{3,19},{4,20},{5,21},{6,22},{7,23},{8,24},{9,... | collective-permute-start | bytes 368648 | tf_op jit(solution)/shard_map/ppermute | solution.py:102
  42.6 18.4 %collective-permute-start.37 = (bf16[48,1536]{1,0:T(8,128)(2,1)S(1)}, bf16[48,1536]{1,0:T(8,128)(2,1)S(1)}, u32[]{:S(2)}, u32[]{:S(2)}) collective-permute-start(bf16[48,1536]{1,0:T(8,128)(2,1)S(1)} %constant_dynamic-slice_fusion.11), channel_id=1, source_target_pairs={{0,16},{1,17},{2,18},{3,19},{4,20},{5,21},{6,22},{7,23},{8,24},{9,... | collective-permute-start | bytes 442376 | tf_op jit(solution)/shard_map/ppermute | solution.py:102
  52.6 26.0 %collective-permute-start.16 = (bf16[4,144,384]{2,1,0:T(8,128)(2,1)S(1)}, bf16[4,144,384]{2,1,0:T(8,128)(2,1)S(1)}, u32[]{:S(2)}, u32[]{:S(2)}) collective-permute-start(bf16[4,144,384]{2,1,0:T(8,128)(2,1)S(1)} %pad_maximum_fusion.3.refs_0_), channel_id=1, source_target_pairs={{0,2},{1,3},{2,0},{3,1},{4,6},{5,7},{6,4},{7,5},{8,10},{9,11},{10,... | collective-permute-start | bytes 1327112 | tf_op jit(solution)/shard_map/ppermute | solution.py:102
  61.0 14.8 %collective-permute-start.26 = (bf16[4,96,384]{2,1,0:T(8,128)(2,1)S(1)}, bf16[4,96,384]{2,1,0:T(8,128)(2,1)S(1)}, u32[]{:S(2)}, u32[]{:S(2)}) collective-permute-start(bf16[4,96,384]{2,1,0:T(8,128)(2,1)S(1)} %pad_maximum_fusion.4.refs_0_), channel_id=1, source_target_pairs={{0,2},{1,3},{2,0},{3,1},{4,6},{5,7},{6,4},{7,5},{8,10},{9,11},{10,... | collective-permute-start | bytes 884744 | tf_op jit(solution)/shard_map/ppermute | solution.py:102
  61.1 14.7 %collective-permute-start.27 = (bf16[4,96,384]{2,1,0:T(8,128)(2,1)S(1)}, bf16[4,96,384]{2,1,0:T(8,128)(2,1)S(1)}, u32[]{:S(2)}, u32[]{:S(2)}) collective-permute-start(bf16[4,96,384]{2,1,0:T(8,128)(2,1)S(1)} %pad_maximum_fusion.4.refs_0_), channel_id=1, source_target_pairs={{0,4},{1,5},{2,6},{3,7},{4,0},{5,1},{6,2},{7,3},{8,12},{9,13},{10,... | collective-permute-start | bytes 884744 | tf_op jit(solution)/shard_map/ppermute | solution.py:102
  62.7 14.7 %collective-permute-start.29 = (bf16[4,96,384]{2,1,0:T(8,128)(2,1)S(1)}, bf16[4,96,384]{2,1,0:T(8,128)(2,1)S(1)}, u32[]{:S(2)}, u32[]{:S(2)}) collective-permute-start(bf16[4,96,384]{2,1,0:T(8,128)(2,1)S(1)} %pad_maximum_fusion.4.refs_0_), channel_id=1, source_target_pairs={{0,1},{1,0},{2,3},{3,2},{4,5},{5,4},{6,7},{7,6},{8,9},{9,8},{10,11... | collective-permute-start | bytes 884744 | tf_op jit(solution)/shard_map/ppermute | solution.py:102
  75.9 15.9 %collective-permute-start.3 = (bf16[4,160,384]{2,1,0:T(8,128)(2,1)S(1)}, bf16[4,160,384]{2,1,0:T(8,128)(2,1)S(1)}, u32[]{:S(2)}, u32[]{:S(2)}) collective-permute-start(bf16[4,160,384]{2,1,0:T(8,128)(2,1)S(1)} %pad_maximum_fusion.2.refs_0_), channel_id=1, source_target_pairs={{0,2},{1,3},{2,0},{3,1},{4,6},{5,7},{6,4},{7,5},{8,10},{9,11},{10,... | collective-permute-start | bytes 1474568 | tf_op jit(solution)/shard_map/ppermute | solution.py:102
  78.2 20.4 %collective-permute-start.4 = (bf16[4,160,384]{2,1,0:T(8,128)(2,1)S(1)}, bf16[4,160,384]{2,1,0:T(8,128)(2,1)S(1)}, u32[]{:S(2)}, u32[]{:S(2)}) collective-permute-start(bf16[4,160,384]{2,1,0:T(8,128)(2,1)S(1)} %pad_maximum_fusion.2.refs_0_), channel_id=1, source_target_pairs={{0,4},{1,5},{2,6},{3,7},{4,0},{5,1},{6,2},{7,3},{8,12},{9,13},{10,... | collective-permute-start | bytes 1474568 | tf_op jit(solution)/shard_map/ppermute | solution.py:102
  78.7 20.8 %collective-permute-start.6 = (bf16[4,160,384]{2,1,0:T(8,128)(2,1)S(1)}, bf16[4,160,384]{2,1,0:T(8,128)(2,1)S(1)}, u32[]{:S(2)}, u32[]{:S(2)}) collective-permute-start(bf16[4,160,384]{2,1,0:T(8,128)(2,1)S(1)} %pad_maximum_fusion.2.refs_0_), channel_id=1, source_target_pairs={{0,1},{1,0},{2,3},{3,2},{4,5},{5,4},{6,7},{7,6},{8,9},{9,8},{10,11... | collective-permute-start | bytes 1474568 | tf_op jit(solution)/shard_map/ppermute | solution.py:102
  88.0 16.9 %collective-permute-start.28 = (bf16[4,96,384]{2,1,0:T(8,128)(2,1)S(1)}, bf16[4,96,384]{2,1,0:T(8,128)(2,1)S(1)}, u32[]{:S(2)}, u32[]{:S(2)}) collective-permute-start(bf16[4,96,384]{2,1,0:T(8,128)(2,1)S(1)} %broadcast_select_fusion.4), channel_id=1, source_target_pairs={{0,4},{1,3},{2,6},{3,1},{4,0},{5,7},{6,2},{7,5},{8,12},{9,11},{10,... | collective-permute-start | bytes 884744 | tf_op jit(solution)/shard_map/ppermute | solution.py:102
  90.2 18.0 %collective-permute-start.39 = (bf16[4,48,1536]{2,1,0:T(8,128)(2,1)S(1)}, bf16[4,48,1536]{2,1,0:T(8,128)(2,1)S(1)}, u32[]{:S(2)}, u32[]{:S(2)}) collective-permute-start(bf16[4,48,1536]{2,1,0:T(8,128)(2,1)S(1)} %pad_maximum_fusion.refs_0_), channel_id=1, source_target_pairs={{0,2},{1,3},{2,0},{3,1},{4,6},{5,7},{6,4},{7,5},{8,10},{9,11},{10,... | collective-permute-start | bytes 1769480 | tf_op jit(solution)/shard_map/ppermute | solution.py:102
  91.8 25.9 %collective-permute-start.40 = (bf16[4,48,1536]{2,1,0:T(8,128)(2,1)S(1)}, bf16[4,48,1536]{2,1,0:T(8,128)(2,1)}, u32[]{:S(2)}, u32[]{:S(2)}) collective-permute-start(bf16[4,48,1536]{2,1,0:T(8,128)(2,1)S(1)} %pad_maximum_fusion.refs_0_), channel_id=1, source_target_pairs={{0,4},{1,5},{2,6},{3,7},{4,0},{5,1},{6,2},{7,3},{8,12},{9,13},{10,... | collective-permute-start | bytes 1769480 | tf_op jit(solution)/shard_map/ppermute | solution.py:102
  98.6 20.6 %collective-permute-start.49 = (bf16[4,192,384]{2,1,0:T(8,128)(2,1)S(1)}, bf16[4,192,384]{2,1,0:T(8,128)(2,1)S(1)}, u32[]{:S(2)}, u32[]{:S(2)}) collective-permute-start(bf16[4,192,384]{2,1,0:T(8,128)(2,1)S(1)} %pad_maximum_fusion.1.refs_0_), channel_id=1, source_target_pairs={{0,2},{1,3},{2,0},{3,1},{4,6},{5,7},{6,4},{7,5},{8,10},{9,11},{10,... | collective-permute-start | bytes 1769480 | tf_op jit(solution)/shard_map/ppermute | solution.py:102
  104.9 20.8 %collective-permute-start.50 = (bf16[4,192,384]{2,1,0:T(8,128)(2,1)S(1)}, bf16[4,192,384]{2,1,0:T(8,128)(2,1)}, u32[]{:S(2)}, u32[]{:S(2)}) collective-permute-start(bf16[4,192,384]{2,1,0:T(8,128)(2,1)S(1)} %pad_maximum_fusion.1.refs_0_), channel_id=1, source_target_pairs={{0,4},{1,5},{2,6},{3,7},{4,0},{5,1},{6,2},{7,3},{8,12},{9,13},{10,... | collective-permute-start | bytes 1769480 | tf_op jit(solution)/shard_map/ppermute | solution.py:102
  107.0 23.3 %collective-permute-start.18 = (bf16[4,144,384]{2,1,0:T(8,128)(2,1)S(1)}, bf16[4,144,384]{2,1,0:T(8,128)(2,1)S(1)}, u32[]{:S(2)}, u32[]{:S(2)}) collective-permute-start(bf16[4,144,384]{2,1,0:T(8,128)(2,1)S(1)} %broadcast_select_fusion.3), channel_id=1, source_target_pairs={{0,4},{1,3},{2,6},{3,1},{4,0},{5,7},{6,2},{7,5},{8,12},{9,11},{10,... | collective-permute-start | bytes 1327112 | tf_op jit(solution)/shard_map/ppermute | solution.py:102
  108.2 22.5 %collective-permute-start.20 = (bf16[4,144,384]{2,1,0:T(8,128)(2,1)S(1)}, bf16[4,144,384]{2,1,0:T(8,128)(2,1)S(1)}, u32[]{:S(2)}, u32[]{:S(2)}) collective-permute-start(bf16[4,144,384]{2,1,0:T(8,128)(2,1)S(1)} %copy-done.4), channel_id=1, source_target_pairs={{0,1},{1,0},{2,3},{3,2},{4,5},{5,4},{6,7},{7,6},{8,9},{9,8},{10,11... | collective-permute-start | bytes 1327112 | tf_op jit(solution)/shard_map/ppermute | solution.py:102
  125.7 31.2 %collective-permute-start.42 = (bf16[4,48,1536]{2,1,0:T(8,128)(2,1)S(1)}, bf16[4,48,1536]{2,1,0:T(8,128)(2,1)S(1)}, u32[]{:S(2)}, u32[]{:S(2)}) collective-permute-start(bf16[4,48,1536]{2,1,0:T(8,128)(2,1)S(1)} %pad_maximum_fusion.refs_0_), channel_id=1, source_target_pairs={{0,1},{1,0},{2,3},{3,2},{4,5},{5,4},{6,7},{7,6},{8,9},{9,8},{10,11... | collective-permute-start | bytes 1769480 | tf_op jit(solution)/shard_map/ppermute | solution.py:102
  125.7 31.2 %collective-permute-start.52 = (bf16[4,192,384]{2,1,0:T(8,128)(2,1)S(1)}, bf16[4,192,384]{2,1,0:T(8,128)(2,1)S(1)}, u32[]{:S(2)}, u32[]{:S(2)}) collective-permute-start(bf16[4,192,384]{2,1,0:T(8,128)(2,1)S(1)} %pad_maximum_fusion.1.refs_0_), channel_id=1, source_target_pairs={{0,1},{1,0},{2,3},{3,2},{4,5},{5,4},{6,7},{7,6},{8,9},{9,8},{10,11... | collective-permute-start | bytes 1769480 | tf_op jit(solution)/shard_map/ppermute | solution.py:102
  139.2 21.5 %collective-permute-start.41 = (bf16[4,48,1536]{2,1,0:T(8,128)(2,1)S(1)}, bf16[4,48,1536]{2,1,0:T(8,128)(2,1)}, u32[]{:S(2)}, u32[]{:S(2)}) collective-permute-start(bf16[4,48,1536]{2,1,0:T(8,128)(2,1)S(1)} %broadcast_select_fusion.1), channel_id=1, source_target_pairs={{0,4},{1,3},{2,6},{3,1},{4,0},{5,7},{6,2},{7,5},{8,12},{9,11},{10,... | collective-permute-start | bytes 1769480 | tf_op jit(solution)/shard_map/ppermute | solution.py:102
  164.7 16.9 %collective-permute-start.33 = (bf16[1,512,768]{2,1,0:T(8,128)(2,1)}, bf16[1,512,768]{2,1,0:T(8,128)(2,1)}, u32[]{:S(2)}, u32[]{:S(2)}) collective-permute-start(bf16[1,512,768]{2,1,0:T(8,128)(2,1)} %fusion.29), channel_id=1, source_target_pairs={{0,1},{1,0},{2,3},{3,2},{4,5},{5,4},{6,7},{7,6},{8,9},{9,8},{10,11... | collective-permute-start | bytes 2359304 | tf_op jit(solution)/shard_map/ppermute | solution.py:102
  165.1 17.9 %collective-permute-start.10 = (bf16[1,512,768]{2,1,0:T(8,128)(2,1)}, bf16[1,512,768]{2,1,0:T(8,128)(2,1)}, u32[]{:S(2)}, u32[]{:S(2)}) collective-permute-start(bf16[1,512,768]{2,1,0:T(8,128)(2,1)} %fusion.28), channel_id=1, source_target_pairs={{0,1},{1,0},{2,3},{3,2},{4,5},{5,4},{6,7},{7,6},{8,9},{9,8},{10,11... | collective-permute-start | bytes 2359304 | tf_op jit(solution)/shard_map/ppermute | solution.py:102
  166.3 18.9 %collective-permute-start.11 = (bf16[1,512,768]{2,1,0:T(8,128)(2,1)}, bf16[1,512,768]{2,1,0:T(8,128)(2,1)S(1)}, u32[]{:S(2)}, u32[]{:S(2)}) collective-permute-start(bf16[1,512,768]{2,1,0:T(8,128)(2,1)} %fusion.25), channel_id=1, source_target_pairs={{0,1},{1,0},{2,3},{3,2},{4,5},{5,4},{6,7},{7,6},{8,9},{9,8},{10,11... | collective-permute-start | bytes 2359304 | tf_op jit(solution)/shard_map/ppermute | solution.py:102
  176.2 24.6 %collective-permute-start.34 = (bf16[1,512,768]{2,1,0:T(8,128)(2,1)}, bf16[1,512,768]{2,1,0:T(8,128)(2,1)S(1)}, u32[]{:S(2)}, u32[]{:S(2)}) collective-permute-start(bf16[1,512,768]{2,1,0:T(8,128)(2,1)} %fusion.26), channel_id=1, source_target_pairs={{0,1},{1,0},{2,3},{3,2},{4,5},{5,4},{6,7},{7,6},{8,9},{9,8},{10,11... | collective-permute-start | bytes 2359304 | tf_op jit(solution)/shard_map/ppermute | solution.py:102
  292.0 54.6 %collective-permute-start.56 = (bf16[1,512,768]{2,1,0:T(8,128)(2,1)}, bf16[1,512,768]{2,1,0:T(8,128)(2,1)}, u32[]{:S(2)}, u32[]{:S(2)}) collective-permute-start(bf16[1,512,768]{2,1,0:T(8,128)(2,1)} %slice.199), channel_id=1, source_target_pairs={{0,1},{1,0},{2,3},{3,2},{4,5},{5,4},{6,7},{7,6},{8,9},{9,8},{10,11... | collective-permute-start | bytes 2359304 | tf_op jit(solution)/shard_map/ppermute | solution.py:102
  302.1 57.4 %collective-permute-start.57 = (bf16[1,512,768]{2,1,0:T(8,128)(2,1)}, bf16[1,512,768]{2,1,0:T(8,128)(2,1)}, u32[]{:S(2)}, u32[]{:S(2)}) collective-permute-start(bf16[1,512,768]{2,1,0:T(8,128)(2,1)} %slice.201), channel_id=1, source_target_pairs={{0,1},{1,0},{2,3},{3,2},{4,5},{5,4},{6,7},{7,6},{8,9},{9,8},{10,11... | collective-permute-start | bytes 2359304 | tf_op jit(solution)/shard_map/ppermute | solution.py:102
  302.7 23.9 %collective-permute-start.75 = (bf16[768,384]{1,0:T(8,128)(2,1)}, bf16[768,384]{1,0:T(8,128)(2,1)}, u32[]{:S(2)}, u32[]{:S(2)}) collective-permute-start(bf16[768,384]{1,0:T(8,128)(2,1)} %convolution_convert_fusion.10), channel_id=1, source_target_pairs={{0,1},{1,0},{2,3},{3,2},{4,5},{5,4},{6,7},{7,6},{8,9},{9,8},{10,11... | collective-permute-start | bytes 1769480 | tf_op jit(solution)/shard_map/ppermute | solution.py:102
  307.5 44.9 %collective-permute-start.59 = (bf16[1,512,768]{2,1,0:T(8,128)(2,1)}, bf16[1,512,768]{2,1,0:T(8,128)(2,1)}, u32[]{:S(2)}, u32[]{:S(2)}) collective-permute-start(bf16[1,512,768]{2,1,0:T(8,128)(2,1)} %slice.205), channel_id=1, source_target_pairs={{0,1},{1,0},{2,3},{3,2},{4,5},{5,4},{6,7},{7,6},{8,9},{9,8},{10,11... | collective-permute-start | bytes 2359304 | tf_op jit(solution)/shard_map/ppermute | solution.py:102
  329.1 19.4 %collective-permute-start.58 = (bf16[1,512,768]{2,1,0:T(8,128)(2,1)S(1)}, bf16[1,512,768]{2,1,0:T(8,128)(2,1)S(1)}, u32[]{:S(2)}, u32[]{:S(2)}) collective-permute-start(bf16[1,512,768]{2,1,0:T(8,128)(2,1)S(1)} %copy-done.56), channel_id=1, source_target_pairs={{0,1},{1,0},{2,3},{3,2},{4,5},{5,4},{6,7},{7,6},{8,9},{9,8},{10,11... | collective-permute-start | bytes 2359304 | tf_op jit(solution)/shard_map/ppermute | solution.py:102
  345.7 85.0 %collective-permute-start.107 = (bf16[768,1536]{1,0:T(8,128)(2,1)}, bf16[768,1536]{1,0:T(8,128)(2,1)}, u32[]{:S(2)}, u32[]{:S(2)}) collective-permute-start(bf16[768,1536]{1,0:T(8,128)(2,1)} %convolution_convert_fusion.1), channel_id=1, source_target_pairs={{0,1},{1,0},{2,3},{3,2},{4,5},{5,4},{6,7},{7,6},{8,9},{9,8},{10,11... | collective-permute-start | bytes 7077896 | tf_op jit(solution)/shard_map/ppermute | solution.py:102
  346.5 38.0 %collective-permute-start.78 = (bf16[4,48,384]{2,1,0:T(8,128)(2,1)}, bf16[4,48,384]{2,1,0:T(8,128)(2,1)}, u32[]{:S(2)}, u32[]{:S(2)}) collective-permute-start(bf16[4,48,384]{2,1,0:T(8,128)(2,1)} %get-tuple-element.113), channel_id=1, source_target_pairs={{0,4},{1,5},{2,6},{3,7},{4,0},{5,1},{6,2},{7,3},{8,12},{9,13},{10,... | collective-permute-start | bytes 442376 | tf_op jit(solution)/shard_map/ppermute | solution.py:102
  348.5 37.6 %collective-permute-start.77 = (bf16[4,48,384]{2,1,0:T(8,128)(2,1)}, bf16[4,48,384]{2,1,0:T(8,128)(2,1)}, u32[]{:S(2)}, u32[]{:S(2)}) collective-permute-start(bf16[4,48,384]{2,1,0:T(8,128)(2,1)} %get-tuple-element.112), channel_id=1, source_target_pairs={{0,2},{1,3},{2,0},{3,1},{4,6},{5,7},{6,4},{7,5},{8,10},{9,11},{10,... | collective-permute-start | bytes 442376 | tf_op jit(solution)/shard_map/ppermute | solution.py:102
  388.3 32.5 %collective-permute-start.91 = (bf16[768,768]{1,0:T(8,128)(2,1)S(1)}, bf16[768,768]{1,0:T(8,128)(2,1)S(1)}, u32[]{:S(2)}, u32[]{:S(2)}) collective-permute-start(bf16[768,768]{1,0:T(8,128)(2,1)S(1)} %fusion.23), channel_id=1, source_target_pairs={{0,1},{1,0},{2,3},{3,2},{4,5},{5,4},{6,7},{7,6},{8,9},{9,8},{10,11... | collective-permute-start | bytes 3538952 | tf_op jit(solution)/shard_map/ppermute | solution.py:102
  411.5 23.6 %collective-permute-start.115 = (bf16[3072,384]{1,0:T(8,128)(2,1)S(1)}, bf16[3072,384]{1,0:T(8,128)(2,1)S(1)}, u32[]{:S(2)}, u32[]{:S(2)}) collective-permute-start(bf16[3072,384]{1,0:T(8,128)(2,1)S(1)} %copy-done.98), channel_id=1, source_target_pairs={{0,1},{1,0},{2,3},{3,2},{4,5},{5,4},{6,7},{7,6},{8,9},{9,8},{10,11... | collective-permute-start | bytes 7077896 | tf_op jit(solution)/shard_map/ppermute | solution.py:102
  414.8 28.0 %collective-permute-start.60 = (bf16[768,1152]{1,0:T(8,128)(2,1)S(1)}, bf16[768,1152]{1,0:T(8,128)(2,1)S(1)}, u32[]{:S(2)}, u32[]{:S(2)}) collective-permute-start(bf16[768,1152]{1,0:T(8,128)(2,1)S(1)} %fusion.6), channel_id=1, source_target_pairs={{0,1},{1,0},{2,3},{3,2},{4,5},{5,4},{6,7},{7,6},{8,9},{9,8},{10,11... | collective-permute-start | bytes 5308424 | tf_op jit(solution)/shard_map/ppermute | solution.py:102
  434.1 25.8 %collective-permute-start.108 = (bf16[4,48,1536]{2,1,0:T(8,128)(2,1)S(1)}, bf16[4,48,1536]{2,1,0:T(8,128)(2,1)S(1)}, u32[]{:S(2)}, u32[]{:S(2)}) collective-permute-start(bf16[4,48,1536]{2,1,0:T(8,128)(2,1)S(1)} %dynamic-slice_bitcast_fusion.1), channel_id=1, source_target_pairs={{0,2},{1,5},{2,0},{3,7},{4,6},{5,1},{6,4},{7,3},{8,10},{9,13},{10,... | collective-permute-start | bytes 1769480 | tf_op jit(solution)/shard_map/ppermute | solution.py:102
  437.2 25.0 %collective-permute-start.116 = (bf16[4,192,384]{2,1,0:T(8,128)(2,1)S(1)}, bf16[4,192,384]{2,1,0:T(8,128)(2,1)S(1)}, u32[]{:S(2)}, u32[]{:S(2)}) collective-permute-start(bf16[4,192,384]{2,1,0:T(8,128)(2,1)S(1)} %dynamic-slice_bitcast_fusion), channel_id=1, source_target_pairs={{0,2},{1,5},{2,0},{3,7},{4,6},{5,1},{6,4},{7,3},{8,10},{9,13},{10,... | collective-permute-start | bytes 1769480 | tf_op jit(solution)/shard_map/ppermute | solution.py:102
  460.2 23.3 %collective-permute-start.110 = (bf16[4,48,1536]{2,1,0:T(8,128)(2,1)S(1)}, bf16[4,48,1536]{2,1,0:T(8,128)(2,1)S(1)}, u32[]{:S(2)}, u32[]{:S(2)}) collective-permute-start(bf16[4,48,1536]{2,1,0:T(8,128)(2,1)S(1)} %get-tuple-element.92), channel_id=1, source_target_pairs={{0,4},{1,5},{2,6},{3,7},{4,0},{5,1},{6,2},{7,3},{8,12},{9,13},{10,... | collective-permute-start | bytes 1769480 | tf_op jit(solution)/shard_map/ppermute | solution.py:102
  461.2 23.8 %collective-permute-start.109 = (bf16[4,48,1536]{2,1,0:T(8,128)(2,1)S(1)}, bf16[4,48,1536]{2,1,0:T(8,128)(2,1)S(1)}, u32[]{:S(2)}, u32[]{:S(2)}) collective-permute-start(bf16[4,48,1536]{2,1,0:T(8,128)(2,1)S(1)} %get-tuple-element.91), channel_id=1, source_target_pairs={{0,2},{1,3},{2,0},{3,1},{4,6},{5,7},{6,4},{7,5},{8,10},{9,11},{10,... | collective-permute-start | bytes 1769480 | tf_op jit(solution)/shard_map/ppermute | solution.py:102
  462.6 32.2 %collective-permute-start.118 = (bf16[4,192,384]{2,1,0:T(8,128)(2,1)S(1)}, bf16[4,192,384]{2,1,0:T(8,128)(2,1)S(1)}, u32[]{:S(2)}, u32[]{:S(2)}) collective-permute-start(bf16[4,192,384]{2,1,0:T(8,128)(2,1)S(1)} %get-tuple-element.90), channel_id=1, source_target_pairs={{0,4},{1,5},{2,6},{3,7},{4,0},{5,1},{6,2},{7,3},{8,12},{9,13},{10,... | collective-permute-start | bytes 1769480 | tf_op jit(solution)/shard_map/ppermute | solution.py:102
  470.8 25.6 %collective-permute-start.117 = (bf16[4,192,384]{2,1,0:T(8,128)(2,1)S(1)}, bf16[4,192,384]{2,1,0:T(8,128)(2,1)S(1)}, u32[]{:S(2)}, u32[]{:S(2)}) collective-permute-start(bf16[4,192,384]{2,1,0:T(8,128)(2,1)S(1)} %get-tuple-element.89), channel_id=1, source_target_pairs={{0,2},{1,3},{2,0},{3,1},{4,6},{5,7},{6,4},{7,5},{8,10},{9,11},{10,... | collective-permute-start | bytes 1769480 | tf_op jit(solution)/shard_map/ppermute | solution.py:102
  472.3 24.7 %collective-permute-start.66 = (bf16[48,1152]{1,0:T(8,128)(2,1)S(1)}, bf16[48,1152]{1,0:T(8,128)(2,1)S(1)}, u32[]{:S(2)}, u32[]{:S(2)}) collective-permute-start(bf16[48,1152]{1,0:T(8,128)(2,1)S(1)} %get-tuple-element.121), channel_id=1, source_target_pairs={{0,24},{1,25},{2,26},{3,27},{4,28},{5,29},{6,30},{7,31},{8,0},{9,1... | collective-permute-start | bytes 331784 | tf_op jit(solution)/shard_map/ppermute | solution.py:102
  483.5 15.0 %collective-permute-start.65 = (bf16[48,1152]{1,0:T(8,128)(2,1)S(1)}, bf16[48,1152]{1,0:T(8,128)(2,1)S(1)}, u32[]{:S(2)}, u32[]{:S(2)}) collective-permute-start(bf16[48,1152]{1,0:T(8,128)(2,1)S(1)} %get-tuple-element.122), channel_id=1, source_target_pairs={{0,16},{1,17},{2,18},{3,19},{4,20},{5,21},{6,22},{7,23},{8,24},{9,... | collective-permute-start | bytes 331784 | tf_op jit(solution)/shard_map/ppermute | solution.py:102
  496.4 20.1 %collective-permute-start.112 = (bf16[48,1536]{1,0:T(8,128)(2,1)S(1)}, bf16[48,1536]{1,0:T(8,128)(2,1)S(1)}, u32[]{:S(2)}, u32[]{:S(2)}) collective-permute-start(bf16[48,1536]{1,0:T(8,128)(2,1)S(1)} %get-tuple-element.119), channel_id=1, source_target_pairs={{0,16},{1,17},{2,18},{3,19},{4,20},{5,21},{6,22},{7,23},{8,24},{9,... | collective-permute-start | bytes 442376 | tf_op jit(solution)/shard_map/ppermute | solution.py:102
  497.0 19.4 %collective-permute-start.111 = (bf16[48,1536]{1,0:T(8,128)(2,1)S(1)}, bf16[48,1536]{1,0:T(8,128)(2,1)S(1)}, u32[]{:S(2)}, u32[]{:S(2)}) collective-permute-start(bf16[48,1536]{1,0:T(8,128)(2,1)S(1)} %get-tuple-element.117), channel_id=1, source_target_pairs={{0,8},{1,9},{2,10},{3,11},{4,12},{5,13},{6,14},{7,15},{8,16},{9,17... | collective-permute-start | bytes 442376 | tf_op jit(solution)/shard_map/ppermute | solution.py:102
  498.7 17.9 %collective-permute-start.121 = (bf16[192,384]{1,0:T(8,128)(2,1)S(1)}, bf16[192,384]{1,0:T(8,128)(2,1)S(1)}, u32[]{:S(2)}, u32[]{:S(2)}) collective-permute-start(bf16[192,384]{1,0:T(8,128)(2,1)S(1)} %get-tuple-element.115), channel_id=1, source_target_pairs={{0,24},{1,25},{2,26},{3,27},{4,28},{5,29},{6,30},{7,31},{8,0},{9,1... | collective-permute-start | bytes 442376 | tf_op jit(solution)/shard_map/ppermute | solution.py:102
  501.2 20.2 %collective-permute-start.120 = (bf16[192,384]{1,0:T(8,128)(2,1)S(1)}, bf16[192,384]{1,0:T(8,128)(2,1)S(1)}, u32[]{:S(2)}, u32[]{:S(2)}) collective-permute-start(bf16[192,384]{1,0:T(8,128)(2,1)S(1)} %get-tuple-element.116), channel_id=1, source_target_pairs={{0,16},{1,17},{2,18},{3,19},{4,20},{5,21},{6,22},{7,23},{8,24},{9,... | collective-permute-start | bytes 442376 | tf_op jit(solution)/shard_map/ppermute | solution.py:102
  504.0 17.4 %collective-permute-start.119 = (bf16[192,384]{1,0:T(8,128)(2,1)S(1)}, bf16[192,384]{1,0:T(8,128)(2,1)S(1)}, u32[]{:S(2)}, u32[]{:S(2)}) collective-permute-start(bf16[192,384]{1,0:T(8,128)(2,1)S(1)} %get-tuple-element.114), channel_id=1, source_target_pairs={{0,8},{1,9},{2,10},{3,11},{4,12},{5,13},{6,14},{7,15},{8,16},{9,17... | collective-permute-start | bytes 442376 | tf_op jit(solution)/shard_map/ppermute | solution.py:102
  (191 other events, 1702.5 us)
